TPU v7x, 128 devices: a whole 4x4x4 slice. The times are simulated.
128 devices in a mesh: cyl: 4 (over z_lo, core), scen: 32 (over y, x, z_hi).
Axes of the slice: x: 4, y: 4, z: 4 (z_hi: 2, z_lo: 2; z = z_hi * 2 + z_lo), core: 2. Of those that a mesh axis runs over, the one named last changes fastest.
Arguments:
- costs: float32 [2048, 20480], P('scen'), may hold values from -6 to 6
- rhs: float32 [2048, 4096], P('scen'), may hold values from -6 to 6
- multipliers: float32 [2048, 16384], P('scen'), may hold values from -4 to 4
- xbar_first_in: float32 [8192], replicated, may hold values from 0 to 1
- xbar_node_in: float32 [48, 8192], replicated, may hold values from 0 to 1
- prox_weights: float32 [4], replicated, may hold values from 0.5 to 4
- start_primal: float32 [2048, 20480], P('scen'), may hold values from 0 to 1
- start_dual: float32 [2048, 4096], P('scen'), may hold values from 0 to 1
- recourse_blocks: bfloat16 [32, 3, 128, 128], replicated, may hold values from -0.3125 to 0.3125
- block_pattern: int32 [32, 3], replicated, may hold values from 0 to 159, as said below
- node_of: int32 [2048], P('scen'), may hold values from 0 to 47, as said below
- pdhg_counts: int32 [4, 2048], P('cyl', 'scen'), may hold values from 3 to 6, as said below
Outputs:
- primal: float32 [4, 2048, 20480], P('cyl', 'scen')
- dual: float32 [4, 2048, 4096], P('cyl', 'scen')
- xbar_first: float32 [8192], replicated
- xbar_node: float32 [48, 8192], replicated
- new_multipliers: float32 [2048, 16384], P('scen')
- objectives: float32 [4], replicated
Inputs may be any that keep to these rules, and one draw needn't show every extreme that they name: `block_pattern`: block column 0 of block row r is 128 + r mod (32); the other 2 of a row are distinct block columns below 128. `node_of`: every node has at least one scenario. `pdhg_counts`: some entry equals 6.
All inputs are finite; a program needn't handle non-finite values.
Results may differ from a plain program's by a relative error of at most 0.00081.
Values sent between devices are 32-bit elements; how exact they have to be, the bound alone decides.
No kernel may reach another device: no remote copies, remote signals or barrier semaphores. Data moves between devices by JAX's collectives and lax.ppermute only.
A program may use at most 128 MiB of HBM per device.

v0:
```python
import jax
import jax.numpy as jnp
from jax import lax
from jax.sharding import PartitionSpec as P

N1 = 8192
N2 = 8192
NNA = 16384
M = 4096
NY = 4096
NZ = 20480
BLK = 128
K = 3
RB = 32
CB = 160
Q = 96
NODES = 48


TAU = 0.4
SIGMA = 0.4


def broadcast(block, axis, owner):
    block = jnp.where(lax.axis_index(axis) == owner, block, jnp.zeros_like(block))
    return lax.psum(block, axis)


def apply_blocks(ext, recourse_blocks, block_pattern):
    count = ext.shape[0]
    cols = block_pattern.reshape(-1)
    tiles = jnp.take(ext.reshape(count, CB, BLK), cols, axis=1)
    flat = recourse_blocks.reshape(Q, BLK, BLK)
    out = jnp.einsum("sqj,qij->sqi", tiles, flat, preferred_element_type=jnp.float32)
    return out.reshape(count, RB, K, BLK).sum(axis=2).reshape(count, M)


def apply_transpose(dual_low, recourse_blocks, block_pattern):
    count = dual_low.shape[0]
    cols = block_pattern.reshape(-1)
    spread = jnp.broadcast_to(dual_low.reshape(count, RB, 1, BLK), (count, RB, K, BLK)).reshape(
        count, Q, BLK
    )
    flat = recourse_blocks.reshape(Q, BLK, BLK)
    contrib = jnp.einsum("sqi,qij->sqj", spread, flat, preferred_element_type=jnp.float32)
    total = jnp.zeros((count, CB, BLK), jnp.float32).at[:, cols, :].add(contrib)
    return total.reshape(count, NZ)


def node_averages(decisions, node_hot, scen_total):
    first_part = jnp.sum(decisions[:, :N1], axis=0)
    node_part = jnp.dot(
        node_hot.T,
        decisions[:, N1:],
        precision=lax.Precision.HIGHEST,
        preferred_element_type=jnp.float32,
    )
    tally = jnp.sum(node_hot, axis=0)
    first_sum, node_sum, tally = lax.psum((first_part, node_part, tally), "scen")
    xbar_first = first_sum / scen_total
    xbar_node = node_sum / tally[:, None]
    return (xbar_first, xbar_node)


def updated_weights(multipliers, decisions, xbar_first, xbar_node, node_hot, hub_rho):
    rows = decisions.shape[0]
    own_node = jnp.dot(
        node_hot, xbar_node, precision=lax.Precision.HIGHEST, preferred_element_type=jnp.float32
    )
    average = jnp.concatenate([jnp.broadcast_to(xbar_first[None, :], (rows, N1)), own_node], axis=1)
    return multipliers + hub_rho * (decisions - average)


def body(
    costs,
    rhs,
    multipliers,
    xbar_first_in,
    xbar_node_in,
    prox_weights,
    start_primal,
    start_dual,
    recourse_blocks,
    block_pattern,
    node_of,
    pdhg_counts,
):
    rows = costs.shape[0]
    scen_total = rows * lax.axis_size("scen")
    node_hot = (node_of[:, None] == jnp.arange(NODES, dtype=jnp.int32)[None, :]).astype(jnp.float32)
    own_node = jnp.dot(
        node_hot, xbar_node_in, precision=lax.Precision.HIGHEST, preferred_element_type=jnp.float32
    )
    gradient = costs + jnp.concatenate([multipliers, jnp.zeros((rows, NY), jnp.float32)], axis=1)
    target = jnp.concatenate(
        [
            jnp.broadcast_to(xbar_first_in[None, :], (rows, N1)),
            own_node,
            jnp.zeros((rows, NY), jnp.float32),
        ],
        axis=1,
    )
    mask = (jnp.arange(NZ) < NNA).astype(jnp.float32)
    rho_vec = prox_weights[lax.axis_index("cyl")] * mask
    counts = pdhg_counts[0]

    def turn(step, state):
        primal_now, dual_now = state
        back = apply_transpose(dual_now.astype(jnp.bfloat16), recourse_blocks, block_pattern)
        fresh = jnp.clip(
            (primal_now - TAU * (gradient - back) + TAU * rho_vec * target) / (1.0 + TAU * rho_vec),
            0.0,
            1.0,
        )
        ext = (2.0 * fresh - primal_now).astype(jnp.bfloat16)
        image = apply_blocks(ext, recourse_blocks, block_pattern)
        dual_new = jnp.maximum(0.0, dual_now + SIGMA * (rhs - image))
        live = (step < counts)[:, None]
        return (jnp.where(live, fresh, primal_now), jnp.where(live, dual_new, dual_now))

    primal_end, dual_end = lax.fori_loop(0, jnp.max(counts), turn, (start_primal, start_dual))
    hub_rho = prox_weights[0]
    decisions = primal_end[:, :NNA]
    own_first, own_node_avg = node_averages(decisions, node_hot, scen_total)
    own_weights = updated_weights(
        multipliers, decisions, own_first, own_node_avg, node_hot, hub_rho
    )
    packed = jnp.concatenate([own_weights.reshape(-1), own_first, own_node_avg.reshape(-1)])
    received = broadcast(packed, "cyl", 0)
    weight_len = rows * NNA
    new_multipliers = received[:weight_len].reshape(rows, NNA)
    xbar_first = received[weight_len : weight_len + N1]
    xbar_node = received[weight_len + N1 :].reshape(NODES, N2)
    local_value = jnp.sum(costs * primal_end) + jnp.sum(new_multipliers * primal_end[:, :NNA])
    total_cost = lax.psum(local_value, "scen") / scen_total
    objectives = lax.all_gather(total_cost.reshape(1), "cyl", axis=0, tiled=True)
    return (primal_end[None], dual_end[None], xbar_first, xbar_node, new_multipliers, objectives)


def solution(mesh):
    return jax.shard_map(
        body,
        mesh=mesh,
        in_specs=(
            P("scen", None),
            P("scen", None),
            P("scen", None),
            P(),
            P(),
            P(),
            P("scen", None),
            P("scen", None),
            P(),
            P(),
            P("scen"),
            P("cyl", "scen"),
        ),
        out_specs=(P("cyl", "scen", None), P("cyl", "scen", None), P(), P(), P("scen", None), P()),
        check_vma=False,
    )
```

profile of v0, /device:TPU:1, one launch (start us, length us, event | category | flops | bytes accessed | tf_op | source)
XLA Modules:
  0.0 946.4 jit_solution(16235586839532567430)
XLA Ops:
  7.3 5.3 copy.83
  16.6 9.6 %maximum_maximum_fusion = (f32[64,20480]{1,0:T(8,128)}, f32[64,20480]{1,0:T(8,128)}) fusion(f32[64,8192]{1,0:T(8,128)} %fusion.26, f32[20480]{0:T(1024)S(1)} %pad.8.clone, f32[20480]{0:T(1024)S(1)} %pad.6.clone, f32[64,20480]{1,0:T(8,128)} %param.14, f32[64,16384]{1,0:T(8,128)} %param.16), kind=kLoop, calls=%fused_computation.36 | loop fusion | flops 3932160 | bytes 22183936 | tf_op jit(solution)/shard_map/concatenate | solution.py:95
  26.1 296.3 %while.14 = (s32[]{:T(128)}, f32[64,20480]{1,0:T(8,128)}, f32[64,4096]{1,0:T(8,128)S(1)}, s32[]{:T(128)}, s32[64]{0:T(128)S(1)}, /*index=5*/s32[32,3]{1,0:T(8,12...) while((s32[]{:T(128)}, f32[64,20480]{1,0:T(8,128)}, ...), condition=%wide.wide.region_4.5_spmd.clone, body=%wide.wide.region_1.4_spmd.clone.sunk | while | flops 420824992 | bytes 92609584 | solution.py:121
  28.7 2.6 fusion.67
  31.3 3.0 broadcast.187
  34.4 15.2 %scatter_fusion = f32[64,160,128]{2,0,1:T(8,128)} fusion(f32[64,160,128]{2,0,1:T(8,128)} %broadcast.187, s32[96]{0:T(128)S(1)} %fusion.66, f32[96,64,128]{2,1,0:T(8,128)} %fusion.67), kind=kCustom, calls=%fused_computation.1.clone.clone.clone.1 | custom fusion | flops 786432 | bytes 9437568 | tf_op jit(solution)/shard_map/while/body/scatter-add | solution.py:46
  50.2 10.5 %fusion.68 = (bf16[8,160,8,128]{3,2,1,0:T(8,128)(2,1)S(1)}, f32[64,20480]{1,0:T(8,128)}) fusion(f32[64,20480]{1,0:T(8,128)} %get-tuple-element.342, f32[20480]{0:T(1024)S(1)} %get-tuple-element.322, f32[64,20480]{1,0:T(8,128)} %get-tuple-element.364, f32[20480]{0:T(1024)S(1)} %get-tuple-element.323, f32[64,20480]{1,0:T(8,128)} %get-tuple-element.363, ...), kind=kLoop, calls=%fused_computation.10.clone.clone.1 | loop fusion | flops 14417920 | bytes 28999744 | tf_op jit(solution)/shard_map/while
  63.0 2.6 gather_fusion
  65.6 5.8 fusion.69
  78.0 2.6 fusion.67
  80.6 3.0 broadcast.187
  83.6 15.2 %scatter_fusion = f32[64,160,128]{2,0,1:T(8,128)} fusion(f32[64,160,128]{2,0,1:T(8,128)} %broadcast.187, s32[96]{0:T(128)S(1)} %fusion.66, f32[96,64,128]{2,1,0:T(8,128)} %fusion.67), kind=kCustom, calls=%fused_computation.1.clone.clone.clone.1 | custom fusion | flops 786432 | bytes 9437568 | tf_op jit(solution)/shard_map/while/body/scatter-add | solution.py:46
  99.5 10.5 %fusion.68 = (bf16[8,160,8,128]{3,2,1,0:T(8,128)(2,1)S(1)}, f32[64,20480]{1,0:T(8,128)}) fusion(f32[64,20480]{1,0:T(8,128)} %get-tuple-element.342, f32[20480]{0:T(1024)S(1)} %get-tuple-element.322, f32[64,20480]{1,0:T(8,128)} %get-tuple-element.364, f32[20480]{0:T(1024)S(1)} %get-tuple-element.323, f32[64,20480]{1,0:T(8,128)} %get-tuple-element.363, ...), kind=kLoop, calls=%fused_computation.10.clone.clone.1 | loop fusion | flops 14417920 | bytes 28999744 | tf_op jit(solution)/shard_map/while
  112.3 2.6 gather_fusion
  114.9 5.8 fusion.69
  127.3 2.6 fusion.67
  129.9 3.0 broadcast.187
  132.9 15.2 %scatter_fusion = f32[64,160,128]{2,0,1:T(8,128)} fusion(f32[64,160,128]{2,0,1:T(8,128)} %broadcast.187, s32[96]{0:T(128)S(1)} %fusion.66, f32[96,64,128]{2,1,0:T(8,128)} %fusion.67), kind=kCustom, calls=%fused_computation.1.clone.clone.clone.1 | custom fusion | flops 786432 | bytes 9437568 | tf_op jit(solution)/shard_map/while/body/scatter-add | solution.py:46
  148.8 10.5 %fusion.68 = (bf16[8,160,8,128]{3,2,1,0:T(8,128)(2,1)S(1)}, f32[64,20480]{1,0:T(8,128)}) fusion(f32[64,20480]{1,0:T(8,128)} %get-tuple-element.342, f32[20480]{0:T(1024)S(1)} %get-tuple-element.322, f32[64,20480]{1,0:T(8,128)} %get-tuple-element.364, f32[20480]{0:T(1024)S(1)} %get-tuple-element.323, f32[64,20480]{1,0:T(8,128)} %get-tuple-element.363, ...), kind=kLoop, calls=%fused_computation.10.clone.clone.1 | loop fusion | flops 14417920 | bytes 28999744 | tf_op jit(solution)/shard_map/while
  164.2 5.8 fusion.69
  176.5 2.6 fusion.67
  179.2 3.0 broadcast.187
  182.2 15.2 %scatter_fusion = f32[64,160,128]{2,0,1:T(8,128)} fusion(f32[64,160,128]{2,0,1:T(8,128)} %broadcast.187, s32[96]{0:T(128)S(1)} %fusion.66, f32[96,64,128]{2,1,0:T(8,128)} %fusion.67), kind=kCustom, calls=%fused_computation.1.clone.clone.clone.1 | custom fusion | flops 786432 | bytes 9437568 | tf_op jit(solution)/shard_map/while/body/scatter-add | solution.py:46
  198.1 10.5 %fusion.68 = (bf16[8,160,8,128]{3,2,1,0:T(8,128)(2,1)S(1)}, f32[64,20480]{1,0:T(8,128)}) fusion(f32[64,20480]{1,0:T(8,128)} %get-tuple-element.342, f32[20480]{0:T(1024)S(1)} %get-tuple-element.322, f32[64,20480]{1,0:T(8,128)} %get-tuple-element.364, f32[20480]{0:T(1024)S(1)} %get-tuple-element.323, f32[64,20480]{1,0:T(8,128)} %get-tuple-element.363, ...), kind=kLoop, calls=%fused_computation.10.clone.clone.1 | loop fusion | flops 14417920 | bytes 28999744 | tf_op jit(solution)/shard_map/while
  213.5 5.8 fusion.69
  225.8 2.6 fusion.67
  228.4 3.0 broadcast.187
  231.5 15.2 %scatter_fusion = f32[64,160,128]{2,0,1:T(8,128)} fusion(f32[64,160,128]{2,0,1:T(8,128)} %broadcast.187, s32[96]{0:T(128)S(1)} %fusion.66, f32[96,64,128]{2,1,0:T(8,128)} %fusion.67), kind=kCustom, calls=%fused_computation.1.clone.clone.clone.1 | custom fusion | flops 786432 | bytes 9437568 | tf_op jit(solution)/shard_map/while/body/scatter-add | solution.py:46
  247.4 10.5 %fusion.68 = (bf16[8,160,8,128]{3,2,1,0:T(8,128)(2,1)S(1)}, f32[64,20480]{1,0:T(8,128)}) fusion(f32[64,20480]{1,0:T(8,128)} %get-tuple-element.342, f32[20480]{0:T(1024)S(1)} %get-tuple-element.322, f32[64,20480]{1,0:T(8,128)} %get-tuple-element.364, f32[20480]{0:T(1024)S(1)} %get-tuple-element.323, f32[64,20480]{1,0:T(8,128)} %get-tuple-element.363, ...), kind=kLoop, calls=%fused_computation.10.clone.clone.1 | loop fusion | flops 14417920 | bytes 28999744 | tf_op jit(solution)/shard_map/while
  262.8 5.8 fusion.69
  275.1 2.6 fusion.67
  277.7 3.0 broadcast.187
  280.8 15.2 %scatter_fusion = f32[64,160,128]{2,0,1:T(8,128)} fusion(f32[64,160,128]{2,0,1:T(8,128)} %broadcast.187, s32[96]{0:T(128)S(1)} %fusion.66, f32[96,64,128]{2,1,0:T(8,128)} %fusion.67), kind=kCustom, calls=%fused_computation.1.clone.clone.clone.1 | custom fusion | flops 786432 | bytes 9437568 | tf_op jit(solution)/shard_map/while/body/scatter-add | solution.py:46
  296.6 10.5 %fusion.68 = (bf16[8,160,8,128]{3,2,1,0:T(8,128)(2,1)S(1)}, f32[64,20480]{1,0:T(8,128)}) fusion(f32[64,20480]{1,0:T(8,128)} %get-tuple-element.342, f32[20480]{0:T(1024)S(1)} %get-tuple-element.322, f32[64,20480]{1,0:T(8,128)} %get-tuple-element.364, f32[20480]{0:T(1024)S(1)} %get-tuple-element.323, f32[64,20480]{1,0:T(8,128)} %get-tuple-element.363, ...), kind=kLoop, calls=%fused_computation.10.clone.clone.1 | loop fusion | flops 14417920 | bytes 28999744 | tf_op jit(solution)/shard_map/while
  312.0 5.8 fusion.69
  322.5 4.2 fusion.22
  328.6 155.7 %all-reduce.2 = (f32[48]{0:T(128)S(1)}, f32[8192]{0:T(1024)S(1)}) all-reduce(f32[48]{0:T(128)S(1)} %convert_reduce_fusion, f32[8192]{0:T(1024)S(1)} %slice_reduce_fusion), channel_id=1, replica_groups=mesh['cyl'=4,'scen'=32] {'scen'}, use_global_device_ids=true, to_apply=%region_9.10 | all-reduce | flops 8240 | bytes 65920 | tf_op jit(solution)/shard_map/psum | solution.py:59
  484.3 178.3 %all-reduce.6.cloned.1.call-done = f32[48,8192]{1,0:T(8,128)} async-done(((f32[48,8192]{1,0:T(8,128)}), f32[48,8192]{1,0:T(8,128)}) %all-reduce.6.cloned.1.call-update) | async-done | bytes 1572880 | tf_op jit(solution)/shard_map/psum | solution.py:59
  662.6 2.7 fusion.25
  665.3 3.5 fusion.21
  670.6 5.4 maximum_select_fusion
  676.1 6.0 multiply_reduce_fusion
  682.1 134.5 %all-reduce.8.cloned.1.call-done = f32[1449984]{0:T(1024)} async-done(((f32[1449984]{0:T(1024)}), f32[1449984]{0:T(1024)}) %all-reduce.8.cloned.1.call-update) | async-done | bytes 5799952 | tf_op jit(solution)/shard_map/psum | solution.py:26
  816.6 4.5 slice.46
  821.1 4.9 reshape.109
  826.0 5.3 multiply_reduce_fusion.1
  833.2 82.4 %psum.39 = f32[]{:T(128)} all-reduce(f32[]{:T(128)S(6)} %add.63), channel_id=1, replica_groups=mesh['cyl'=4,'scen'=32] {'scen'}, use_global_device_ids=true, to_apply=%region_13.14 | all-reduce | flops 1 | bytes 8 | tf_op jit(solution)/shard_map/psum | solution.py:135
  917.0 19.8 %all-reduce.1 = f32[4]{0:T(128)} all-reduce(f32[4]{0:T(128)S(1)} %dynamic-update-slice), channel_id=1, replica_groups=mesh['cyl'=4,'scen'=32] {'cyl'}, use_global_device_ids=true, to_apply=%add.1 | all-reduce | flops 4 | bytes 32
  (129 shorter events, 74.9 us)
Async XLA Ops:
  7.2 6.4 copy-start
  7.2 5.7 copy-start.8
  7.2 5.8 copy-start.10
  7.2 5.4 copy-start.9
  7.2 6.3 copy-start.11
  7.2 655.3 %all-reduce.6.cloned.1.call-start = ((), (), s32[]{:S(2)}) async-start(), calls=%async_computation | async-start | bytes 3145728 | tf_op jit(solution)/shard_map/psum | solution.py:59
  12.6 3.3 copy-start.12
  12.7 13.4 %copy-start.7 = (s32[32,3]{1,0:T(8,128)}, s32[32,3]{1,0:T(8,128)S(1)}, u32[]{:S(2)}) copy-start(s32[32,3]{1,0:T(8,128)S(1)} %copy.40) | copy-start | bytes 1156
  16.6 9.6 %copy-start.4 = (f32[64,4096]{1,0:T(8,128)S(1)}, f32[64,4096]{1,0:T(8,128)}, u32[]{:S(2)}) copy-start(f32[64,4096]{1,0:T(8,128)} %param.21) | copy-start | bytes 3145732
  26.8 1.9 copy-start.2
  76.1 1.9 copy-start.2
  125.4 1.9 copy-start.2
  174.6 1.9 copy-start.2
  223.9 1.9 copy-start.2
  273.2 1.9 copy-start.2
  322.5 342.8 %copy-start.3 = (f32[64,4096]{1,0:T(8,128)}, f32[64,4096]{1,0:T(8,128)S(1)}, u32[]{:S(2)}) copy-start(f32[64,4096]{1,0:T(8,128)S(1)} %get-tuple-element.66) | copy-start | bytes 3145732
  326.7 489.9 %all-reduce.8.cloned.1.call-start = ((), (), s32[]{:S(2)}) async-start(), calls=%async_computation.1 | async-start | bytes 11599872 | tf_op jit(solution)/shard_map/psum | solution.py:26
  662.6 2.7 copy-start.5
  668.8 1.4 copy-start.6
  826.0 6.6 copy-start.13
  826.0 110.8 %slice-start = ((f32[1449984]{0:T(1024)}), f32[393216]{0:T(1024)S(1)}, s32[]{:S(2)}) async-start(f32[1449984]{0:T(1024)} %all-reduce.8.cloned.1.call-done), calls=%async_computation.2 | async-start | bytes 3145728 | tf_op jit(solution)/shard_map/slice | solution.py:133
  826.0 113.6 %copy-start.1 = (f32[48,8192]{1,0:T(8,128)S(1)}, f32[48,8192]{1,0:T(8,128)}, u32[]{:S(2)}) copy-start(f32[48,8192]{1,0:T(8,128)} %param.18) | copy-start | bytes 4718596
Sparse Core Ops, SparseCore 0:
  326.8 335.7 all-reduce.5
  676.2 140.3 all-reduce.7
where the time goes:
time: 949 us; the launch traced here: 946 us
  waiting for transfers between devices  313 us (33%)
  blocking collectives  258 us (27%)
  other arithmetic  216 us (23%)
  local copies, waits for them, and re-layouts  79.2 us (8%)
  matrix products  59.7 us (6%)
  between operations  16.2 us (2%)
    psum x1, waiting for transfers between devices, node_averages(): lax.psum((first_part, node_part, tally), 'scen')  178 us
    psum x1, blocking collectives, node_averages(): lax.psum((first_part, node_part, tally), 'scen')  156 us
    psum x1, waiting for transfers between devices, broadcast(): return lax.psum(block, axis)  134 us
    scatter-add x6, other arithmetic, apply_transpose(): total = jnp.zeros((count, CB, BLK), jnp.float32).at[:, cols, :].add(contrib)  91.3 us
    psum x1, blocking collectives, body(): total_cost = lax.psum(local_value, 'scen') / scen_total  82.4 us
    while x6, other arithmetic  63.2 us
    dot_general x6, matrix products, apply_blocks(): jnp.einsum('sqj,qij->sqi', tiles, flat, preferred_element_type=jnp.float32)  34.7 us
    unnamed x1, blocking collectives  19.8 us
  transfers between devices with their start and end apart: 2, of which 2 were waited for; matrix products, arithmetic and copies ran while one was open for 1% of the time, Pallas kernels for 0%

commit v1 on v0

v1 whole, which is shorter than its diff:
```python
import functools

import jax
import jax.numpy as jnp
from jax import lax
from jax.experimental import pallas as pl
from jax.experimental.pallas import tpu as pltpu
from jax.sharding import PartitionSpec as P

N1 = 8192
N2 = 8192
NNA = 16384
M = 4096
NZ = 20480
BLK = 128
RB = 32
Q = 96
NODES = 48
SCEN = 2048
ROWS = 64
N_CYL = 4
GROUPS = 32
HALF = 24
SHARD = 32
CB1 = N1 // BLK
CBA = NNA // BLK
CHUNK = 2048
PER = CHUNK // BLK
ZERO_SLOT = 96
ALL = ("scen", "cyl")

TAU = 0.4
SIGMA = 0.4

ANY = pl.BlockSpec(memory_space=pl.ANY)
VM = pl.BlockSpec(memory_space=pltpu.VMEM)
SM = pl.BlockSpec(memory_space=pltpu.SMEM)


def cols(c):
    return pl.ds(pl.multiple_of(c * BLK, BLK), BLK)


def split(value):
    high = value.astype(jnp.bfloat16)
    return high, (value - high.astype(jnp.float32)).astype(jnp.bfloat16)


def dot(a, b):
    return jnp.dot(a, b, preferred_element_type=jnp.float32)


def one_hot(node_ref):
    lanes = lax.broadcasted_iota(jnp.int32, (ROWS, BLK), 1)
    return (node_ref[...] == lanes).astype(jnp.float32)


def solve_kernel(
    pattern, prox, costs, rhs, mult, first_in, node_in, start, start_dual, blocks, node_rows, counts,
    primal, dual, weights, sums, cost_sum,
    head, coupled, slot, free, dup_to, dup_from,
    z, d, gc, gm, back, ext, u, uq, rh, raw, wide, tall, nodes, firsts, shards,
    sem, osem,
):
    cyl = lax.axis_index("cyl")
    rhos = (prox[0], prox[cyl])
    invs = [1.0 / (1.0 + TAU * jnp.full((8, BLK), rho, jnp.float32)) for rho in rhos]
    inv = [jnp.broadcast_to(one[:1], (ROWS, BLK)) for one in invs]
    coef = [TAU * one for one in inv]
    pull = [TAU * rho * one for rho, one in zip(rhos, inv)]
    part = [slice(0, ROWS), slice(ROWS, 2 * ROWS)]

    def copy(src, dst, k):
        return pltpu.make_async_copy(src, dst, sem.at[k])

    block_copy = copy(blocks, raw, 0)
    dual_copies = [copy(start_dual, u.at[part[g]], 1 + g) for g in range(2)]
    node_copy = copy(node_in, nodes, 3)
    first_copy = copy(first_in, firsts, 4)
    rhs_copy = copy(rhs, rh, 5)
    chunk_copies = []
    for n in range(NZ // CHUNK):
        at = pl.ds(n * CHUNK, CHUNK)
        group = [copy(costs.at[:, at], gc.at[:, at], 6 + 4 * n)]
        if n * CHUNK < NNA:
            group.append(copy(mult.at[:, at], gm.at[:, at], 7 + 4 * n))
        for g in range(2):
            group.append(copy(start.at[:, at], z.at[part[g], at], 8 + 4 * n + g))
        chunk_copies.append(group)
    for one in [block_copy, *dual_copies, *sum(chunk_copies[NNA // CHUNK:], []), node_copy, first_copy]:
        one.start()
    for group in chunk_copies[: NNA // CHUNK]:
        for one in group:
            one.start()
    rhs_copy.start()

    def clear(c, carry):
        slot[c] = -1
        return carry

    lax.fori_loop(0, CBA, clear, 0, unroll=8)

    def note(r, dups):
        for k in range(2):
            c = pattern[r, k + 1]
            s = 2 * r + k
            was = slot[c]
            seen = (was >= 0).astype(jnp.int32)
            lead = jnp.where(was >= 0, was, s)
            slot[c] = lead
            head[s] = lead
            dup_to[dups] = lead
            dup_from[dups] = s
            dups = dups + seen
        return dups

    dups = lax.fori_loop(0, RB, note, 0)

    def place(c, carry):
        used, unused = carry
        was = slot[c]
        hit = (was >= 0).astype(jnp.int32)
        coupled[used] = c
        slot[CBA + used] = was
        free[unused] = c
        return used + hit, unused + 1 - hit

    used, _ = lax.fori_loop(0, CBA, place, (0, 0), unroll=4)

    def fill(j, carry):
        coupled[j] = free[64 + j - used]
        slot[CBA + j] = ZERO_SLOT
        return carry

    lax.fori_loop(used, 64, fill, 0)

    back[:, cols(ZERO_SLOT)] = jnp.zeros((2 * ROWS, BLK), jnp.float32)
    block_copy.wait()

    def arrange(r, carry):
        for k in range(3):
            one = raw[3 * r + k]
            wide[r, :, k * BLK : (k + 1) * BLK] = one
            tall[r, k * BLK : (k + 1) * BLK, :] = one.T
        return carry

    lax.fori_loop(0, RB, arrange, 0, unroll=4)
    for one in dual_copies:
        one.wait()

    def low_dual(r, carry):
        uq[:, cols(r)] = u[:, cols(r)].astype(jnp.bfloat16)
        return carry

    lax.fori_loop(0, RB, low_dual, 0, unroll=4)
    for one in sum(chunk_copies[NNA // CHUNK:], []):
        one.wait()

    def pick(g, t, new, old):
        if t is None:
            return new
        return jnp.where(counts[part[g], :] > t, new, old)

    def spread(t):
        for r in range(RB):
            product = dot(uq[:, r * BLK : (r + 1) * BLK], wide[r])
            back[:, 2 * r * BLK : (2 * r + 2) * BLK] = product[:, BLK:]
            at = slice(NNA + r * BLK, NNA + (r + 1) * BLK)
            for g in range(2):
                now = z[part[g], at]
                fresh = jnp.clip(now + TAU * (product[part[g], :BLK] - gc[:, at]), 0.0, 1.0)
                ext[part[g], (64 + r) * BLK : (65 + r) * BLK] = (fresh + fresh - now).astype(jnp.bfloat16)
                z[part[g], at] = pick(g, t, fresh, now)

        def merge(k, carry):
            to = cols(dup_to[k])
            back[:, to] += back[:, cols(dup_from[k])]
            return carry

        lax.fori_loop(0, dups, merge, 0)

    def touch(t):
        def step(j, carry):
            c = cols(coupled[j])
            s = cols(slot[CBA + j])
            for g in range(2):
                now = z[part[g], c]
                fresh = jnp.clip(now * inv[g] + back[part[g], s] * coef[g] + d[part[g], c], 0.0, 1.0)
                ext[part[g], s] = (fresh + fresh - now).astype(jnp.bfloat16)
                z[part[g], c] = pick(g, t, fresh, now)
            return carry

        lax.fori_loop(0, 64, step, 0, unroll=8)

    def image(t):
        for r in range(RB):
            at = slice(r * BLK, (r + 1) * BLK)
            left = [ext[:, (64 + r) * BLK : (65 + r) * BLK], ext[:, cols(head[2 * r])], ext[:, cols(head[2 * r + 1])]]
            product = dot(jnp.concatenate(left, axis=1), tall[r])
            for g in range(2):
                old = u[part[g], at]
                new = jnp.maximum(0.0, old + SIGMA * (rh[:, at] - product[part[g]]))
                new = pick(g, t, new, old)
                u[part[g], at] = new
                uq[part[g], at] = new.astype(jnp.bfloat16)

    spread(None)
    node_copy.wait()
    first_copy.wait()
    hot = one_hot(node_rows)
    hot_low = hot.astype(jnp.bfloat16)[:, :NODES]
    for n in range(NNA // CHUNK):
        for one in chunk_copies[n]:
            one.wait()

        def prepare(c, carry):
            if n * CHUNK < N1:
                target = jnp.broadcast_to(firsts[pl.ds(c, 1), :], (ROWS, BLK))
            else:
                high, low = split(nodes[:, cols(c - CB1)])
                target = dot(hot_low, high) + dot(hot_low, low)
            gradient = gc[:, cols(c)] + gm[:, cols(c)]
            for g in range(2):
                d[part[g], cols(c)] = pull[g] * target - coef[g] * gradient
            return carry

        lax.fori_loop(n * PER, (n + 1) * PER, prepare, 0, unroll=4)
    rhs_copy.wait()

    def plain(t, carry):
        touch(None)
        image(None)
        spread(None)
        return carry

    def chosen(t, carry):
        touch(t)
        image(t)
        spread(t + 1)
        return carry

    lax.fori_loop(0, 2, plain, 0)
    lax.fori_loop(2, 5, chosen, 0)
    touch(5)

    def loose(j, carry):
        c = cols(free[j])
        for g in range(2):
            now = z[part[g], c]
            shift = d[part[g], c]
            for t in range(6):
                fresh = jnp.clip(now * inv[g] + shift, 0.0, 1.0)
                now = pick(g, t if t > 2 else None, fresh, now)
            z[part[g], c] = now
        return carry

    lax.fori_loop(0, 64, loose, 0, unroll=2)

    def send(src, dst, k):
        one = pltpu.make_async_copy(src, dst, osem.at[k])
        one.start()
        return one

    outs = [send(z.at[part[1]], primal.at[0], 0)]
    image(5)
    outs.append(send(u.at[part[1]], dual.at[0], 1))

    hot_turned = hot.T[:NODES].astype(jnp.bfloat16)
    tally = jnp.sum(hot, axis=0, keepdims=True)

    def shard(m, carry):
        block = cyl * PER + m
        high, low = split(z[part[0], cols(CB1 + block)])
        node_sum = dot(hot_turned, high) + dot(hot_turned, low)
        first_sum = jnp.sum(z[part[0], cols(block)], axis=0, keepdims=True)
        tail = jnp.concatenate([first_sum, tally, jnp.zeros((SHARD - HALF - 2, BLK), jnp.float32)], axis=0)
        for half in range(2):
            shards[2 * m + half, :HALF, :] = node_sum[half * HALF : (half + 1) * HALF]
            shards[2 * m + half, HALF:, :] = tail
        return carry

    lax.fori_loop(0, PER, shard, 0, unroll=2)
    outs.append(send(shards, sums, 2))

    hub_rho = rhos[0]
    for n in range(NNA // CHUNK):
        at = slice(n * CHUNK, (n + 1) * CHUNK)
        gm[:, at] = gm[:, at] + hub_rho * z[part[0], at]
        outs.append(send(gm.at[:, at], weights.at[:, at], 3 + n))
    total = jnp.zeros((ROWS, BLK), jnp.float32)

    def cost(c, acc):
        return acc + gc[:, cols(c)] * z[part[1], cols(c)]

    total = lax.fori_loop(0, NZ // BLK, cost, total, unroll=4)
    cost_sum[...] = jnp.sum(total.reshape(ROWS // 8, 8, BLK), axis=0)
    for one in outs:
        one.wait()


def solve(pattern, prox, costs, rhs, mult, first_in, node_in, start, start_dual, blocks, node_rows, counts):
    f32, bf16 = jnp.float32, jnp.bfloat16
    both = 2 * ROWS
    V = pltpu.VMEM
    return pl.pallas_call(
        solve_kernel,
        out_shape=[
            jax.ShapeDtypeStruct((1, ROWS, NZ), f32),
            jax.ShapeDtypeStruct((1, ROWS, M), f32),
            jax.ShapeDtypeStruct((ROWS, NNA), f32),
            jax.ShapeDtypeStruct((GROUPS, SHARD, BLK), f32),
            jax.ShapeDtypeStruct((8, BLK), f32),
        ],
        in_specs=[SM, SM] + [ANY] * 8 + [VM, VM],
        out_specs=[ANY] * 4 + [VM],
        scratch_shapes=[
            pltpu.SMEM((72,), jnp.int32),
            pltpu.SMEM((136,), jnp.int32),
            pltpu.SMEM((2 * CBA + 8,), jnp.int32),
            pltpu.SMEM((136,), jnp.int32),
            pltpu.SMEM((72,), jnp.int32),
            pltpu.SMEM((72,), jnp.int32),
            V((both, NZ), f32),
            V((both, NNA), f32),
            V((ROWS, NZ), f32),
            V((ROWS, NNA), f32),
            V((both, 97 * BLK), f32),
            V((both, 97 * BLK), bf16),
            V((both, M), f32),
            V((both, M), bf16),
            V((ROWS, M), f32),
            V((Q, BLK, BLK), bf16),
            V((RB, BLK, 3 * BLK), bf16),
            V((RB, 3 * BLK, BLK), bf16),
            V((NODES, N2), f32),
            V((CB1, BLK), f32),
            V((GROUPS, SHARD, BLK), f32),
            pltpu.SemaphoreType.DMA((48,)),
            pltpu.SemaphoreType.DMA((12,)),
        ],
        compiler_params=pltpu.CompilerParams(vmem_limit_bytes=62 * 2**20),
        name="solve",
    )(pattern, prox, costs, rhs, mult, first_in, node_in, start, start_dual, blocks, node_rows, counts)


def average_kernel(sums, out):
    half = lax.axis_index("scen") % 2
    total = sums[0]
    for i in range(1, GROUPS):
        total = total + sums[i]
    tally = jnp.broadcast_to(total[HALF + 1 : HALF + 2], (HALF, BLK))
    lanes = lax.broadcasted_iota(jnp.int32, (HALF, BLK), 1)
    wanted = lax.broadcasted_iota(jnp.int32, (HALF, BLK), 0) + half * HALF
    count = jnp.sum(jnp.where(lanes == wanted, tally, 0.0), axis=1, keepdims=True)
    low = total[:HALF] / count
    rest = total[HALF:] * (1.0 / SCEN)
    top = low[: SHARD // 2]
    bottom = jnp.concatenate([low[SHARD // 2 :], rest], axis=0)

    def put(i, carry):
        for c in range(N_CYL):
            out[i * N_CYL + c] = bottom if c % 2 else top
        return carry

    lax.fori_loop(0, GROUPS, put, 0, unroll=2)


def average(sums):
    return pl.pallas_call(
        average_kernel,
        out_shape=jax.ShapeDtypeStruct((GROUPS * N_CYL, SHARD // 2, BLK), jnp.float32),
        in_specs=[VM],
        out_specs=VM,
        name="average",
    )(sums)


def update_kernel(
    prox, mine, other, weights, primal, node_rows, cost_sum,
    multipliers, first_out, node_out, value,
    shards, w, x, nodes, sem, osem,
):
    cyl = lax.axis_index("cyl")
    core = cyl % 2
    rho = prox[0]

    def copy(src, dst, k):
        return pltpu.make_async_copy(src, dst, sem.at[k])

    parts = [copy(mine, shards.at[core], 0), copy(other, shards.at[1 - core], 1)]
    for one in parts:
        one.start()
    chunks = []
    for n in range(NNA // CHUNK):
        at = pl.ds(n * CHUNK, CHUNK)
        group = [copy(weights.at[:, at], w.at[:, at], 2 + 2 * n), copy(primal.at[0, :, at], x.at[:, at], 3 + 2 * n)]
        for one in group:
            one.start()
        chunks.append(group)
    hot = one_hot(node_rows).astype(jnp.bfloat16)[:, :NODES]
    for one in parts:
        one.wait()

    outs = []
    acc = jnp.zeros((ROWS, BLK), jnp.float32)
    for n in range(NNA // CHUNK):
        for one in chunks[n]:
            one.wait()

        def step(m, acc):
            if n * CHUNK < N1:
                block = n * PER + m
                lead = 8 * m + n
                row = shards[1, lead, pl.ds(HALF - SHARD // 2, 1), :]
                first_out[pl.ds(block, 1), :] = row
                own = jnp.broadcast_to(row, (ROWS, BLK))
            else:
                lead = 8 * m + n - N1 // CHUNK
                nodes_now = jnp.concatenate(
                    [
                        shards[0, lead],
                        shards[1, lead, : HALF - SHARD // 2, :],
                        shards[0, lead + N_CYL],
                        shards[1, lead + N_CYL, : HALF - SHARD // 2, :],
                    ],
                    axis=0,
                )
                nodes[:, cols((n - N1 // CHUNK) * PER + m)] = nodes_now
                high, low = split(nodes_now)
                own = dot(hot, high) + dot(hot, low)
            c = cols(n * PER + m)
            new = w[:, c] - rho * own
            w[:, c] = new
            return acc + new * x[:, c]

        acc = lax.fori_loop(0, PER, step, acc, unroll=4)
        at = pl.ds(n * CHUNK, CHUNK)
        one = pltpu.make_async_copy(w.at[:, at], multipliers.at[:, at], osem.at[n])
        one.start()
        outs.append(one)
    one = pltpu.make_async_copy(nodes, node_out, osem.at[NNA // CHUNK])
    one.start()
    outs.append(one)
    total = jnp.sum(acc) + jnp.sum(cost_sum[...])
    value[...] = jnp.full(value.shape, total, jnp.float32)
    for one in outs:
        one.wait()


def update(prox, mine, other, weights, primal, node_rows, cost_sum):
    f32 = jnp.float32
    V = pltpu.VMEM
    return pl.pallas_call(
        update_kernel,
        out_shape=[
            jax.ShapeDtypeStruct((ROWS, NNA), f32),
            jax.ShapeDtypeStruct((CB1, BLK), f32),
            jax.ShapeDtypeStruct((NODES, N2), f32),
            jax.ShapeDtypeStruct((GROUPS * N_CYL, BLK), f32),
        ],
        in_specs=[SM, ANY, ANY, ANY, ANY, VM, VM],
        out_specs=[ANY, VM, ANY, VM],
        scratch_shapes=[
            V((2, GROUPS * N_CYL, SHARD // 2, BLK), f32),
            V((ROWS, NNA), f32),
            V((ROWS, NNA), f32),
            V((NODES, N2), f32),
            pltpu.SemaphoreType.DMA((24,)),
            pltpu.SemaphoreType.DMA((12,)),
        ],
        compiler_params=pltpu.CompilerParams(vmem_limit_bytes=40 * 2**20),
        name="update",
    )(prox, mine, other, weights, primal, node_rows, cost_sum)


def body(
    costs,
    rhs,
    multipliers,
    xbar_first_in,
    xbar_node_in,
    prox_weights,
    start_primal,
    start_dual,
    recourse_blocks,
    block_pattern,
    node_of,
    pdhg_counts,
):
    hub_counts = lax.all_gather(pdhg_counts, "cyl", axis=0, tiled=True)[0]
    counts = jnp.broadcast_to(jnp.concatenate([hub_counts, pdhg_counts[0]])[:, None], (2 * ROWS, BLK))
    node_rows = jnp.broadcast_to(node_of[:, None], (ROWS, BLK))
    primal, dual, weights, sums, cost_sum = solve(
        block_pattern,
        prox_weights,
        costs,
        rhs,
        multipliers,
        xbar_first_in.reshape(CB1, BLK),
        xbar_node_in,
        start_primal,
        start_dual,
        recourse_blocks.reshape(Q, BLK, BLK),
        node_rows,
        counts,
    )
    gathered = lax.all_to_all(sums, "scen", 0, 0, tiled=True)
    shares = average(gathered)
    mine = lax.all_to_all(shares, ALL, 0, 0, tiled=True)
    other = lax.ppermute(mine, "cyl", [(0, 1), (1, 0), (2, 3), (3, 2)])
    new_multipliers, first, xbar_node, value = update(
        prox_weights, mine, other, weights, primal, node_rows, cost_sum
    )
    values = lax.all_to_all(value, ALL, 0, 0, tiled=True)
    objectives = jnp.sum(values.reshape(GROUPS, N_CYL, BLK)[:, :, 0], axis=0) / SCEN
    return (primal, dual, first.reshape(N1), xbar_node, new_multipliers, objectives)


def solution(mesh):
    return jax.shard_map(
        body,
        mesh=mesh,
        in_specs=(
            P("scen", None),
            P("scen", None),
            P("scen", None),
            P(),
            P(),
            P(),
            P("scen", None),
            P("scen", None),
            P(),
            P(),
            P("scen"),
            P("cyl", "scen"),
        ),
        out_specs=(P("cyl", "scen", None), P("cyl", "scen", None), P(), P(), P("scen", None), P()),
        check_vma=False,
    )
```

time: 949 us -> 133 us (0.14)
  waiting for transfers between devices: 313 us -> 2.29 us
  other arithmetic: 216 us -> 1.39 us
  blocking collectives: 258 us -> 67.4 us
  local copies, waits for them, and re-layouts: 79.2 us -> 8.09 us
  matrix products: 59.7 us -> 0 us
  Pallas kernels: 0 us -> 51.1 us
  between operations: 16.2 us -> 0.69 us
    psum x2 -> x0, waiting for transfers between devices: 313 us -> none  [the longest x1 178 us: node_averages(): lax.psum((first_part, node_part, tally), 'scen')]
    psum x2 -> x0, blocking collectives: 238 us -> none  [the longest x1 156 us: node_averages(): lax.psum((first_part, node_part, tally), 'scen')]
    scatter-add x6 -> x0, other arithmetic: 91.3 us -> none  [apply_transpose(): total = jnp.zeros((count, CB, BLK), jnp.float32).at[:, cols, :].add(contrib)]
    while x6 -> x0, other arithmetic: 63.2 us -> none
    all_to_all x0 -> x3, blocking collectives: none -> 61 us  [the longest x1 24.6 us: body(): mine = lax.all_to_all(shares, ALL, 0, 0, tiled=True)]
    dot_general x15 -> x0, matrix products: 59.7 us -> none  [the longest x6 34.7 us: apply_blocks(): jnp.einsum('sqj,qij->sqi', tiles, flat, preferred_element_type=jnp.float32)]
    pallas_call x0 -> x3, Pallas kernels: none -> 51.1 us  [the longest x1 41.8 us: solve(): pl.pallas_call(solve_kernel, out_shape=[jax.ShapeDtypeStruct((1, ROWS, NZ...]
    reduce_sum x10 -> x1, other arithmetic: 27 us -> 0.15 us  [body(): jnp.sum(values.reshape(GROUPS, N_CYL, BLK)[:, :, 0], axis=0) / SCEN]
  transfers between devices with their start and end apart: 2 -> 1, of which waited for: 2 -> 1; matrix products, arithmetic and copies ran while one was open for 1% -> 0% of each run, Pallas kernels for 0% -> 0%
where the time goes in v1:
time: 133 us; the launch traced here: 132 us
  blocking collectives  67.4 us (51%)
  Pallas kernels  51.1 us (38%)
  local copies, waits for them, and re-layouts  8.09 us (6%)
  waiting for transfers between devices  2.29 us (2%)
  other arithmetic  1.39 us (1%)
    pallas_call x1, Pallas kernels, solve(): pl.pallas_call(solve_kernel, out_shape=[jax.ShapeDtypeStruct((1, ROWS, NZ...  41.8 us
    all_to_all x1, blocking collectives, body(): mine = lax.all_to_all(shares, ALL, 0, 0, tiled=True)  24.6 us
    all_to_all x1, blocking collectives, body(): gathered = lax.all_to_all(sums, 'scen', 0, 0, tiled=True)  23.6 us
    all_to_all x1, blocking collectives, body(): values = lax.all_to_all(value, ALL, 0, 0, tiled=True)  12.8 us
    pallas_call x1, Pallas kernels, update(): pl.pallas_call(update_kernel, out_shape=[jax.ShapeDtypeStruct((ROWS, NNA)...  7.13 us
    all_gather x1, blocking collectives, body(): hub_counts = lax.all_gather(pdhg_counts, 'cyl', axis=0, tiled=True)[0]  6.42 us
    unnamed x11, local copies, waits for them, and re-layouts  6.05 us
  transfers between devices with their start and end apart: 1, of which 1 were waited for; matrix products, arithmetic and copies ran while one was open for 0% of the time, Pallas kernels for 0%

profile of v1, /device:TPU:1, one launch (start us, length us, event | category | flops | bytes accessed | tf_op | source)
XLA Modules:
  0.0 132.1 jit_solution(3766693490448406567)
XLA Ops:
  0.6 6.4 %all-gather = s32[4,1,64]{2,1,0:T(1,128)S(1)} all-gather(s32[1,1,64]{2,1,0:T(1,128)} %bitcast.15), channel_id=1, replica_groups=mesh['cyl'=4,'scen'=32] {'cyl'}, dimensions={0}, use_global_device_ids=true | all-gather | bytes 1280 | tf_op jit(solution)/shard_map/all_gather | solution.py:490
  7.1 1.4 %copy.19.pattern = s32[32,3]{1,0:T(8,128)} copy(s32[32,3]{0,1:T(4,128)} %param.21) | data formatting | bytes 768 | tf_op args[9]
  8.4 0.7 pad_add_fusion
  9.1 1.3 %broadcast_in_dim.4.node_rows = s32[64,128]{1,0:T(8,128)} broadcast(s32[64]{0:T(128)} %param.22), dimensions={0} | broadcast | bytes 33024 | tf_op jit(solution)/shard_map/broadcast_in_dim | solution.py:492
  10.5 0.7 broadcast_in_dim.5.counts
  11.2 41.8 %solve.1 = (f32[1,64,20480]{2,1,0:T(8,128)}, f32[1,64,4096]{2,1,0:T(8,128)}, f32[64,16384]{1,0:T(8,128)}, f32[32,32,128]{2,1,0:T(8,128)}, f32[8,128]{1,0:T(8,128)}) custom-call(s32[32,3]{1,0:T(8,128)} %copy.19.pattern, f32[4]{0:T(128)} %prox.3, f32[64,20480]{1,0:T(8,128)} %costs.1, f32[64,4096]{1,0:T(8,128)} %rhs.1, f32[64,16384]{1,0:T(8,128)} %mult.1, ...), custom_call_target="tpu_custom_call" | custom-call | tf_op jit(solution)/shard_map/solve/pallas_call | solution.py:305
  53.0 0.0 copy-start.2
  53.0 0.0 copy-start.3
  53.0 0.0 copy-start.4
  53.0 23.6 %all_to_all.19.sums = f32[32,32,128]{2,1,0:T(8,128)} all-to-all(f32[32,32,128]{2,1,0:T(8,128)} %get-tuple-element.17), channel_id=1, replica_groups=mesh['cyl'=4,'scen'=32] {'scen'}, dimensions={0} | all-to-all | bytes 1048576 | tf_op jit(solution)/shard_map/all_to_all | solution.py:507
  76.6 2.2 %average.1 = f32[128,16,128]{2,1,0:T(8,128)} custom-call(f32[32,32,128]{2,1,0:T(8,128)} %all_to_all.19.sums), custom_call_target="tpu_custom_call" | custom-call | tf_op jit(solution)/shard_map/average/pallas_call | solution.py:369
  78.8 24.6 %all_to_all.20.mine = f32[128,16,128]{2,1,0:T(8,128)S(1)} all-to-all(f32[128,16,128]{2,1,0:T(8,128)} %average.1), channel_id=1, replica_groups=mesh['cyl'=4,'scen'=32] {'scen','cyl'}, dimensions={0} | all-to-all | bytes 2097152 | tf_op jit(solution)/shard_map/all_to_all | solution.py:509
  103.4 1.2 collective-permute-start
  104.6 2.3 %collective-permute-done.other = f32[128,16,128]{2,1,0:T(8,128)S(1)} collective-permute-done((f32[128,16,128]{2,1,0:T(8,128)S(1)}, f32[128,16,128]{2,1,0:T(8,128)S(1)}, u32[]{:S(2)}, u32[]{:S(2)}) %collective-permute-start) | collective-permute-done | bytes 1048608 | tf_op jit(solution)/shard_map/ppermute | solution.py:510
  106.8 0.0 copy-done.2
  106.8 0.0 copy-done.3
  106.8 0.0 copy-done.4
  106.8 0.0 copy-start
  106.9 2.5 %copy-done = f32[1,64,20480]{2,1,0:T(8,128)S(1)} copy-done((f32[1,64,20480]{2,1,0:T(8,128)S(1)}, f32[1,64,20480]{2,1,0:T(8,128)}, u32[]{:S(2)}) %copy-start) | copy-done | bytes 5242904
  109.3 0.0 copy-start.1
  109.3 2.2 %copy-done.1 = f32[64,16384]{1,0:T(8,128)S(1)} copy-done((f32[64,16384]{1,0:T(8,128)S(1)}, f32[64,16384]{1,0:T(8,128)}, u32[]{:S(2)}) %copy-start.1) | copy-done | bytes 4194328
  111.5 7.1 %update.1 = (f32[64,16384]{1,0:T(8,128)}, f32[64,128]{1,0:T(8,128)}, f32[48,8192]{1,0:T(8,128)}, f32[128,128]{1,0:T(8,128)S(1)}) custom-call(f32[4]{0:T(128)S(1)} %copy-done.4, f32[128,16,128]{2,1,0:T(8,128)S(1)} %all_to_all.20.mine, f32[128,16,128]{2,1,0:T(8,128)S(1)} %collective-permute-done.other, f32[64,16384]{1,0:T(8,128)S(1)} %copy-done.1, ...), custom_call_target="tpu_custom_call" | custom-call | tf_op jit(solution)/shard_map/update/pallas_call | solution.py:453
  118.7 12.8 %all_to_all.21 = f32[128,1,128]{2,1,0:T(1,128)S(1)} all-to-all(f32[128,1,128]{2,1,0:T(1,128)S(1)} %bitcast.11), channel_id=1, replica_groups=mesh['cyl'=4,'scen'=32] {'scen','cyl'}, dimensions={0} | all-to-all | bytes 131072 | tf_op jit(solution)/shard_map/all_to_all | solution.py:514
  131.5 0.1 slice_reduce_fusion
  131.6 0.5 broadcast_multiply_fusion
  (1 shorter events, 0.0 us)
Async XLA Ops:
  53.0 53.9 %copy-start.2 = (s32[64,128]{1,0:T(8,128)S(1)}, s32[64,128]{1,0:T(8,128)}, u32[]{:S(2)}) copy-start(s32[64,128]{1,0:T(8,128)} %broadcast_in_dim.4.node_rows) | copy-start | bytes 98308
  53.0 53.9 %copy-start.3 = (f32[8,128]{1,0:T(8,128)S(1)}, f32[8,128]{1,0:T(8,128)}, u32[]{:S(2)}) copy-start(f32[8,128]{1,0:T(8,128)} %get-tuple-element.19.cost_sum) | copy-start | bytes 12292
  53.0 53.9 %copy-start.4 = (f32[4]{0:T(128)S(1)}, f32[4]{0:T(128)}, u32[]{:S(2)}) copy-start(f32[4]{0:T(128)} %prox.3) | copy-start | bytes 52
  103.4 3.5 %collective-permute-start = (f32[128,16,128]{2,1,0:T(8,128)S(1)}, f32[128,16,128]{2,1,0:T(8,128)S(1)}, u32[]{:S(2)}, u32[]{:S(2)}) collective-permute-start(f32[128,16,128]{2,1,0:T(8,128)S(1)} %all_to_all.20.mine), channel_id=1, source_target_pairs={{0,32},{32,0},{64,96},{96,64},{1,33},{33,1},{65,97},{97,65},{2,34}... | collective-permute-start | bytes 3145736 | tf_op jit(solution)/shard_map/ppermute | solution.py:510
  106.8 2.5 %copy-start = (f32[1,64,20480]{2,1,0:T(8,128)S(1)}, f32[1,64,20480]{2,1,0:T(8,128)}, u32[]{:S(2)}) copy-start(f32[1,64,20480]{2,1,0:T(8,128)} %get-tuple-element.9.primal) | copy-start | bytes 15728644
  109.3 2.2 %copy-start.1 = (f32[64,16384]{1,0:T(8,128)S(1)}, f32[64,16384]{1,0:T(8,128)}, u32[]{:S(2)}) copy-start(f32[64,16384]{1,0:T(8,128)} %get-tuple-element.18.weights) | copy-start | bytes 12582916

commit v2 on v0

v2 whole, which is shorter than its diff:
```python
import functools

import jax
import jax.numpy as jnp
from jax import lax
from jax.experimental import pallas as pl
from jax.experimental.pallas import tpu as pltpu
from jax.sharding import PartitionSpec as P

N1 = 8192
N2 = 8192
NNA = 16384
M = 4096
NZ = 20480
BLK = 128
RB = 32
Q = 96
NODES = 48
SCEN = 2048
ROWS = 64
N_CYL = 4
GROUPS = 32
HALF = 24
SHARD = 32
CB1 = N1 // BLK
CBA = NNA // BLK
CHUNK = 2048
PER = CHUNK // BLK
ZERO_SLOT = 64
VMEM_LIMIT = 62 * 2**20
ALL = ("scen", "cyl")

TAU = 0.4
SIGMA = 0.4

ANY = pl.BlockSpec(memory_space=pl.ANY)
HBM = pl.BlockSpec(memory_space=pltpu.HBM)
VM = pl.BlockSpec(memory_space=pltpu.VMEM)
SM = pl.BlockSpec(memory_space=pltpu.SMEM)


def cols(c):
    return pl.ds(pl.multiple_of(c * BLK, BLK), BLK)


def split(value):
    high = value.astype(jnp.bfloat16)
    return high, (value - high.astype(jnp.float32)).astype(jnp.bfloat16)


def dot(a, b):
    return jnp.dot(a, b, preferred_element_type=jnp.float32)


def down(row):
    row = jnp.broadcast_to(row, (ROWS, ROWS))
    here = lax.broadcasted_iota(jnp.int32, (ROWS, ROWS), 0) == lax.broadcasted_iota(jnp.int32, (ROWS, ROWS), 1)
    return jnp.broadcast_to(jnp.sum(jnp.where(here, row, 0), axis=1, keepdims=True), (ROWS, BLK))


def one_hot(node_row):
    lanes = lax.broadcasted_iota(jnp.int32, (ROWS, BLK), 1)
    return (down(node_row) == lanes).astype(jnp.float32)


def solve_kernel(kind, *refs):
    (pattern, prox, node_of, counts_in, costs, rhs, mult, first_in, node_in, start, start_dual) = refs[:11]
    refs = refs[11:]
    is_hub = kind == "hub"
    if is_hub:
        (blocks, own_in, first_counts, second_counts, third_counts, weights, lagrange) = refs[:7]
        refs = refs[7:]
    else:
        blocks, primal, dual, sums = refs[:4]
        refs = refs[4:]
    (
        head, lead_of, coupled, slot, free, dup_to, dup_from,
        counts, z, z_odd, z_own, z_free, d, gc, gm, back, back_odd, ext, ext_own, u, uq, rh, wide, tall, nodes, firsts,
        extra, sem, osem,
    ) = (*refs[:26], refs[26:-2], *refs[-2:])
    cyl = lax.axis_index("cyl")
    rho = prox[0] if is_hub else prox[cyl]
    inv = jnp.broadcast_to((1.0 / (1.0 + TAU * jnp.full((8, BLK), rho, jnp.float32)))[:1], (ROWS, BLK))
    coef = TAU * inv
    pull = TAU * rho * inv

    def copy(src, dst, k):
        return pltpu.make_async_copy(src, dst, sem.at[k])

    block_copies = []
    for n in range(4):
        at = pl.ds(8 * n, 8)
        group = [copy(blocks.at[at, k], wide.at[at, :, pl.ds(k * BLK, BLK)], 40 + 3 * n + k) for k in range(3)]
        block_copies.append(group)
    dual_copy = copy(start_dual, u, 2)
    node_copy = copy(node_in, nodes, 3)
    first_copy = copy(first_in, firsts, 4)
    rhs_copy = copy(rhs, rh, 5)
    chunk_copies = []
    for n in range(NZ // CHUNK):
        at = pl.ds(n * CHUNK, CHUNK)
        where = z.at[:, at] if n * CHUNK < NNA else z_own.at[:, pl.ds(n * CHUNK - NNA, CHUNK)]
        group = [copy(costs.at[:, at], gc.at[:, at], 6 + 3 * n), copy(start.at[:, at], where, 7 + 3 * n)]
        if n * CHUNK < NNA:
            group.append(copy(mult.at[:, at], gm.at[:, at], 8 + 3 * n))
        chunk_copies.append(group)
    own_copies = sum(chunk_copies[NNA // CHUNK :], [])
    for one in [*sum(block_copies, []), dual_copy, *own_copies, first_copy]:
        one.start()
    for n, group in enumerate(chunk_copies[: NNA // CHUNK]):
        if n == N1 // CHUNK - 1:
            node_copy.start()
        for one in group:
            one.start()
    rhs_copy.start()
    if is_hub:
        own_copy = copy(own_in.at[0], extra[0], 0)
        own_copy.start()

    def clear(c, carry):
        lead_of[c] = -1
        return carry

    lax.fori_loop(0, CBA, clear, 0, unroll=16)

    def note(r, carry):
        used, dups = carry
        for k in range(2):
            c = pattern[k + 1, r]
            s = 2 * r + k
            was = lead_of[c]
            new = (was < 0).astype(jnp.int32)
            lead = jnp.where(was < 0, s, was)
            lead_of[c] = lead
            head[s] = lead
            coupled[used] = c
            slot[used] = s
            dup_to[dups] = lead
            dup_from[dups] = s
            used, dups = used + new, dups + 1 - new
        return used, dups

    used, dups = lax.fori_loop(0, RB, note, (0, 0), unroll=4)

    def place(c, unused):
        free[unused] = c
        return unused + (lead_of[c] < 0).astype(jnp.int32)

    lax.fori_loop(0, CBA, place, 0, unroll=8)

    def fill(j, carry):
        coupled[j] = free[64 + j - used]
        slot[j] = ZERO_SLOT
        return carry

    lax.fori_loop(used, 64, fill, 0)
    if is_hub:
        mine = jnp.where(cyl == 0, counts_in[...], 0)
        counts[...] = down(mine + first_counts[...] + second_counts[...] + third_counts[...])
    else:
        counts[...] = down(counts_in[...])
    hot = one_hot(node_of[...])
    hot_low = hot.astype(jnp.bfloat16)[:, :NODES]
    hot_turned = hot.T[:NODES].astype(jnp.bfloat16)

    for one in (back, back_odd):
        one[:, cols(ZERO_SLOT)] = jnp.zeros((ROWS, BLK), jnp.float32)
    def arrange(r, carry):
        for k in range(3):
            tall[r, k * BLK : (k + 1) * BLK, :] = wide[r, :, k * BLK : (k + 1) * BLK].T
        return carry

    for n in range(4):
        for one in block_copies[n]:
            one.wait()
        lax.fori_loop(8 * n, 8 * n + 8, arrange, 0, unroll=8)
    for one in own_copies:
        one.wait()
    dual_copy.wait()

    def choose(live, new, old):
        return new if live is None else jnp.where(live, new, old)

    def spread(r, low, out, live):
        product = dot(low, wide[r])
        out[:, 2 * r * BLK : (2 * r + 2) * BLK] = product[:, BLK:]
        at = slice(r * BLK, (r + 1) * BLK)
        now = z_own[:, at]
        cost = gc[:, NNA + r * BLK : NNA + (r + 1) * BLK]
        fresh = jnp.clip(now + TAU * (product[:, :BLK] - cost), 0.0, 1.0)
        ext_own[:, at] = (fresh + fresh - now).astype(jnp.bfloat16)
        z_own[:, at] = choose(live, fresh, now)

    def merge(out):
        def step(k, carry):
            to = cols(dup_to[k])
            out[:, to] += out[:, cols(dup_from[k])]
            return carry

        lax.fori_loop(0, dups, step, 0)

    def loose(j, lives):
        c = cols(free[j])
        now = z[:, c]
        shift = d[:, c]
        for t in range(6):
            fresh = jnp.clip(now * inv + shift, 0.0, 1.0)
            now = fresh if t < 3 else jnp.where(lives[t - 3], fresh, now)
        z_free[:, cols(j)] = now

    def touch(before, after, back_in, live, lives, base, loose_count):
        for r in range(RB):
            for k in range(2):
                c = cols(coupled[2 * r + k])
                s = cols(slot[2 * r + k])
                now = before[:, c]
                fresh = jnp.clip(now * inv + back_in[:, s] * coef + d[:, c], 0.0, 1.0)
                ext[:, s] = (fresh + fresh - now).astype(jnp.bfloat16)
                after[:, c] = choose(live, fresh, now)
            if r < loose_count:
                loose(base + r, lives)

    def image(live):
        for r in range(RB):
            at = slice(r * BLK, (r + 1) * BLK)
            left = [ext_own[:, at], ext[:, cols(head[2 * r])], ext[:, cols(head[2 * r + 1])]]
            product = dot(jnp.concatenate(left, axis=1), tall[r])
            old = u[:, at]
            new = choose(live, jnp.maximum(0.0, old + SIGMA * (rh[:, at] - product)), old)
            u[:, at] = new
            uq[:, at] = new.astype(jnp.bfloat16)

    def turn(t, before, after, back_in, back_out, base, loose_count):
        live = counts[...] > t
        lives = [counts[...] > k for k in range(3, 6)]
        touch(before, after, back_in, live, lives, base, loose_count)
        image(live)
        next_live = counts[...] > t + 1
        for r in range(RB):
            spread(r, uq[:, r * BLK : (r + 1) * BLK], back_out, next_live)
        merge(back_out)

    def send(src, dst, k):
        one = pltpu.make_async_copy(src, dst, osem.at[k])
        one.start()
        return one

    def sum_nodes(block):
        high, low = split(z[:, cols(CB1 + block)])
        first = jnp.sum(z[:, cols(block)], axis=0, keepdims=True)
        return dot(hot_turned, high) + dot(hot_turned, low), first

    outs = []
    for r in range(RB):
        spread(r, u[:, r * BLK : (r + 1) * BLK].astype(jnp.bfloat16), back, None)
    merge(back)
    first_copy.wait()
    node_copy.wait()
    for n in range(NNA // CHUNK):
        for one in chunk_copies[n]:
            one.wait()

        def prepare(c, carry):
            if n * CHUNK < N1:
                target = jnp.broadcast_to(firsts[pl.ds(c, 1), :], (ROWS, BLK))
            else:
                high, low = split(nodes[:, cols(c - CB1)])
                target = dot(hot_low, high) + dot(hot_low, low)
            d[:, cols(c)] = pull * target - coef * (gc[:, cols(c)] + gm[:, cols(c)])
            return carry

        lax.fori_loop(n * PER, (n + 1) * PER, prepare, 0, unroll=8)
    rhs_copy.wait()

    def pair(i, carry):
        turn(2 * i, z, z_odd, back, back_odd, 16 * i, 16)
        turn(2 * i + 1, z_odd, z, back_odd, back, 0, 0)
        return carry

    lax.fori_loop(0, 2, pair, 0)
    turn(4, z, z_odd, back, back_odd, 32, 32)
    final = counts[...] > 5
    touch(z_odd, z, back_odd, final, None, 0, 0)

    def put_back(j, carry):
        z[:, cols(free[j])] = z_free[:, cols(j)]
        return carry

    lax.fori_loop(0, 64, put_back, 0, unroll=8)

    if is_hub:
        own_copy.wait()
        own = extra[0]

        def linear(c, acc):
            weight = gm[:, cols(c)] + rho * z[:, cols(c)]
            gm[:, cols(c)] = weight
            return acc + (gc[:, cols(c)] + weight) * own[:, cols(c)]

        def cost(c, acc):
            return acc + gc[:, cols(c)] * own[:, cols(c)]

        total = jnp.zeros((ROWS, BLK), jnp.float32)
        for n in range(NNA // CHUNK):
            total = lax.fori_loop(n * PER, (n + 1) * PER, linear, total, unroll=4)
            at = pl.ds(n * CHUNK, CHUNK)
            outs.append(send(gm.at[:, at], weights.at[:, at], n))
        total = lax.fori_loop(CBA, NZ // BLK, cost, total, unroll=4)
        lagrange[...] = jnp.sum(total.reshape(ROWS // 8, 8, BLK), axis=0)
    else:
        outs += [send(z, primal.at[0, :, pl.ds(0, NNA)], 0), send(z_own, primal.at[0, :, pl.ds(NNA, NZ - NNA)], 6)]
        tally = jnp.sum(hot, axis=0, keepdims=True)
        zeros = jnp.zeros((SHARD - HALF - 2, BLK), jnp.float32)

        image(final)
        outs.append(send(u, dual.at[0], 1))

        def shard(m, carry):
            for c in range(N_CYL):
                block = c * PER + m
                high, low = split(z[:, cols(CB1 + block)])
                node_sum = dot(hot_turned, high) + dot(hot_turned, low)
                first_sum = jnp.sum(z[:, cols(block)], axis=0, keepdims=True)
                tail = jnp.concatenate([first_sum, tally, zeros], axis=0)
                for half in range(2):
                    at = (2 * m + half) * N_CYL + c
                    extra[0][at, :HALF, :] = node_sum[half * HALF : (half + 1) * HALF]
                    extra[0][at, HALF:, :] = tail
            return carry

        for n in range(4):
            lax.fori_loop(4 * n, 4 * n + 4, shard, 0, unroll=4)
            at = pl.ds(GROUPS * n, GROUPS)
            outs.append(send(extra[0].at[at], sums.at[at], 2 + n))
    for one in outs:
        one.wait()


def solve(kind, *args):
    f32, bf16, i32 = jnp.float32, jnp.bfloat16, jnp.int32
    V = pltpu.VMEM
    wide, tall = (RB, BLK, 3 * BLK), (RB, 3 * BLK, BLK)
    shares = (GROUPS * N_CYL, SHARD, BLK)
    if kind == "hub":
        outs = [((ROWS, NNA), f32), ((8, BLK), f32)]
        extra, out_specs, in_more = [V((ROWS, NZ), f32)], [HBM, VM], [HBM, HBM] + [VM] * 3
    else:
        outs = [((1, ROWS, NZ), f32), ((1, ROWS, M), f32), (shares, f32)]
        extra, out_specs, in_more = [V(shares, f32)], [HBM] * 3, [HBM]
    return pl.pallas_call(
        functools.partial(solve_kernel, kind),
        out_shape=[jax.ShapeDtypeStruct(*one) for one in outs],
        in_specs=[SM, SM, VM, VM] + [HBM] * 7 + in_more,
        out_specs=out_specs,
        scratch_shapes=[
            *[pltpu.SMEM((136,), i32)] * 7,
            V((ROWS, BLK), i32),
            V((ROWS, NNA), f32),
            V((ROWS, NNA), f32),
            V((ROWS, M), f32),
            V((ROWS, 64 * BLK), f32),
            V((ROWS, NNA), f32),
            V((ROWS, NZ), f32),
            V((ROWS, NNA), f32),
            V((ROWS, 65 * BLK), f32),
            V((ROWS, 65 * BLK), f32),
            V((ROWS, 65 * BLK), bf16),
            V((ROWS, M), bf16),
            V((ROWS, M), f32),
            V((ROWS, M), bf16),
            V((ROWS, M), f32),
            V(wide, bf16),
            V(tall, bf16),
            V((NODES, N2), f32),
            V((CB1, BLK), f32),
            *extra,
            pltpu.SemaphoreType.DMA((56,)),
            pltpu.SemaphoreType.DMA((8,)),
        ],
        compiler_params=pltpu.CompilerParams(vmem_limit_bytes=VMEM_LIMIT),
        cost_estimate=pl.CostEstimate(flops=10**10, bytes_accessed=4 * 10**7, transcendentals=0),
        name="solve_" + kind,
    )(*args)


def average_kernel(prox, sums, lagrange, out):
    cyl = lax.axis_index("cyl")
    half = lax.axis_index("scen") % 2
    totals = [sums[c] for c in range(N_CYL)]
    for i in range(1, GROUPS):
        totals = [total + sums[i * N_CYL + c] for c, total in enumerate(totals)]
    hub = totals[0]
    tally = jnp.broadcast_to(hub[HALF + 1 : HALF + 2], (HALF, BLK))
    lanes = lax.broadcasted_iota(jnp.int32, (HALF, BLK), 1)
    wanted = lax.broadcasted_iota(jnp.int32, (HALF, BLK), 0) + half * HALF
    count = jnp.sum(jnp.where(lanes == wanted, tally, 0.0), axis=1, keepdims=True)
    low = hub[:HALF] / count
    first = hub[HALF : HALF + 1] * (1.0 / SCEN)
    once = jnp.where(half == 0, first, jnp.zeros_like(first))
    lane = lax.broadcasted_iota(jnp.int32, (1, BLK), 1)
    scalars = jnp.where(lane == cyl, jnp.sum(lagrange[...]), 0.0)
    for c, total in enumerate(totals):
        both = jnp.sum(low * total[:HALF]) + jnp.sum(once * total[HALF : HALF + 1])
        scalars = scalars - jnp.where(lane == c, prox[0] * both, 0.0)
    top = low[: SHARD // 2]
    zeros = jnp.zeros((SHARD - HALF - 2, BLK), jnp.float32)
    bottom = jnp.concatenate([low[SHARD // 2 :], first, scalars, zeros], axis=0)

    def put(i, carry):
        for c in range(N_CYL):
            out[i * N_CYL + c] = bottom if c % 2 else top
        return carry

    lax.fori_loop(0, GROUPS, put, 0, unroll=2)


def average(prox, sums, lagrange):
    return pl.pallas_call(
        average_kernel,
        out_shape=jax.ShapeDtypeStruct((GROUPS * N_CYL, SHARD // 2, BLK), jnp.float32),
        in_specs=[SM, VM, VM],
        out_specs=VM,
        cost_estimate=pl.CostEstimate(flops=10**7, bytes_accessed=4 * 10**6, transcendentals=0),
        name="average",
    )(prox, sums, lagrange)


def fetch_shards(mine, other, shards, sem):
    core = lax.axis_index("cyl") % 2
    parts = [
        pltpu.make_async_copy(mine, shards.at[core], sem.at[0]),
        pltpu.make_async_copy(other, shards.at[1 - core], sem.at[1]),
    ]
    for one in parts:
        one.start()
    return parts


def averages(shards, c, m):
    lead = 2 * N_CYL * m + c
    rest = slice(0, HALF - SHARD // 2)
    pieces = [shards[0, lead], shards[1, lead, rest, :], shards[0, lead + N_CYL], shards[1, lead + N_CYL, rest, :]]
    return jnp.concatenate(pieces, axis=0), shards[1, lead, pl.ds(HALF - SHARD // 2, 1), :]


def update_kernel(
    prox, mine, other, weights, node_of, multipliers, first_out, node_out, objectives, shards, w, nodes, sem, osem
):
    rho = prox[0]
    parts = fetch_shards(mine, other, shards, sem)
    chunks = []
    for n in range(NNA // CHUNK):
        at = pl.ds(n * CHUNK, CHUNK)
        chunks.append(pltpu.make_async_copy(weights.at[:, at], w.at[:, at], sem.at[2 + n]))
        chunks[-1].start()
    hot = one_hot(node_of[...]).astype(jnp.bfloat16)[:, :NODES]
    for one in parts:
        one.wait()
    outs = []
    for n in range(NNA // CHUNK):
        chunks[n].wait()

        def step(m, carry):
            node_avg, first = averages(shards, n % N_CYL, m)
            block = (n % N_CYL) * PER + m
            if n * CHUNK < N1:
                first_out[pl.ds(block, 1), :] = first
                own = jnp.broadcast_to(first, (ROWS, BLK))
            else:
                nodes[:, cols(block)] = node_avg
                high, low = split(node_avg)
                own = dot(hot, high) + dot(hot, low)
            c = cols(n * PER + m)
            w[:, c] = w[:, c] - rho * own
            return carry

        lax.fori_loop(0, PER, step, 0, unroll=8)
        at = pl.ds(n * CHUNK, CHUNK)
        outs.append(pltpu.make_async_copy(w.at[:, at], multipliers.at[:, at], osem.at[n]))
        outs[-1].start()
        if n * CHUNK >= N1:
            at = pl.ds(n * CHUNK - N1, CHUNK)
            outs.append(pltpu.make_async_copy(nodes.at[:, at], node_out.at[:, at], osem.at[n + 4]))
            outs[-1].start()

    def add(i, acc):
        return acc + shards[1, i, 8:, :]

    total = lax.fori_loop(1, GROUPS * N_CYL, add, shards[1, 0, 8:, :], unroll=8)
    lane = lax.broadcasted_iota(jnp.int32, (1, BLK), 1)
    for c in range(N_CYL):
        objectives[c] = jnp.sum(jnp.where(lane == c, total[1:2], 0.0)) * (1.0 / SCEN)
    for one in outs:
        one.wait()


def update(prox, mine, other, weights, node_of):
    f32 = jnp.float32
    V = pltpu.VMEM
    return pl.pallas_call(
        update_kernel,
        out_shape=[
            jax.ShapeDtypeStruct((ROWS, NNA), f32),
            jax.ShapeDtypeStruct((CB1, BLK), f32),
            jax.ShapeDtypeStruct((NODES, N2), f32),
            jax.ShapeDtypeStruct((N_CYL,), f32),
        ],
        in_specs=[SM, ANY, ANY, HBM, VM],
        out_specs=[HBM, VM, HBM, SM],
        scratch_shapes=[
            V((2, GROUPS * N_CYL, SHARD // 2, BLK), f32),
            V((ROWS, NNA), f32),
            V((NODES, N2), f32),
            pltpu.SemaphoreType.DMA((12,)),
            pltpu.SemaphoreType.DMA((12,)),
        ],
        compiler_params=pltpu.CompilerParams(vmem_limit_bytes=VMEM_LIMIT),
        cost_estimate=pl.CostEstimate(flops=10**9, bytes_accessed=2 * 10**7, transcendentals=0),
        name="update",
    )(prox, mine, other, weights, node_of)


def body(
    costs,
    rhs,
    multipliers,
    xbar_first_in,
    xbar_node_in,
    prox_weights,
    start_primal,
    start_dual,
    recourse_blocks,
    block_pattern,
    node_of,
    pdhg_counts,
):
    hub_counts = [lax.ppermute(pdhg_counts, "cyl", [(0, c)]) for c in range(1, N_CYL)]
    pattern = block_pattern.T
    node_row = node_of.reshape(1, ROWS)
    data = (costs, rhs, multipliers, xbar_first_in.reshape(CB1, BLK), xbar_node_in, start_primal, start_dual)
    ints = (pattern, prox_weights, node_row, pdhg_counts)
    primal, dual, sums = solve("own", *ints, *data, recourse_blocks)
    sums, *hub_counts = lax.optimization_barrier((sums, *hub_counts))
    gathered = lax.all_to_all(sums, ALL, 0, 0, tiled=True)
    weights, lagrange = solve("hub", *ints, *data, recourse_blocks, primal, *hub_counts)
    shares = average(prox_weights, gathered, lagrange)
    mine = lax.all_to_all(shares, ALL, 0, 0, tiled=True)
    other = lax.ppermute(mine, "cyl", [(0, 1), (1, 0), (2, 3), (3, 2)])
    new_multipliers, first, xbar_node, objectives = update(prox_weights, mine, other, weights, node_row)
    return (primal, dual, first.reshape(N1), xbar_node, new_multipliers, objectives)


def solution(mesh):
    return jax.shard_map(
        body,
        mesh=mesh,
        in_specs=(
            P("scen", None),
            P("scen", None),
            P("scen", None),
            P(),
            P(),
            P(),
            P("scen", None),
            P("scen", None),
            P(),
            P(),
            P("scen"),
            P("cyl", "scen"),
        ),
        out_specs=(P("cyl", "scen", None), P("cyl", "scen", None), P(), P(), P("scen", None), P()),
        check_vma=False,
    )
```

time: 949 us -> 114 us (0.12)
  waiting for transfers between devices: 313 us -> 6.71 us
  blocking collectives: 258 us -> 24.5 us
  other arithmetic: 216 us -> 0 us
  local copies, waits for them, and re-layouts: 79.2 us -> 1.02 us
  Pallas kernels: 0 us -> 60.5 us
  matrix products: 59.7 us -> 0 us
  starting transfers between devices: 0.08 us -> 19.1 us
  between operations: 16.2 us -> 0.91 us
    psum x2 -> x0, waiting for transfers between devices: 313 us -> none  [the longest x1 178 us: node_averages(): lax.psum((first_part, node_part, tally), 'scen')]
    psum x2 -> x0, blocking collectives: 238 us -> none  [the longest x1 156 us: node_averages(): lax.psum((first_part, node_part, tally), 'scen')]
    scatter-add x6 -> x0, other arithmetic: 91.3 us -> none  [apply_transpose(): total = jnp.zeros((count, CB, BLK), jnp.float32).at[:, cols, :].add(contrib)]
    while x6 -> x0, other arithmetic: 63.2 us -> none
    pallas_call x0 -> x4, Pallas kernels: none -> 60.5 us  [the longest x2 51.1 us: solve(): pl.pallas_call(functools.partial(solve_kernel, kind), out_shape=[jax.Shap...]
    dot_general x15 -> x0, matrix products: 59.7 us -> none  [the longest x6 34.7 us: apply_blocks(): jnp.einsum('sqj,qij->sqi', tiles, flat, preferred_element_type=jnp.float32)]
    reduce_sum x10 -> x0, other arithmetic: 27 us -> none  [the longest x6 13.9 us: apply_blocks(): return out.reshape(count, RB, K, BLK).sum(axis=2).reshape(count, M)]
    all_to_all x0 -> x1, blocking collectives: none -> 24.5 us  [body(): mine = lax.all_to_all(shares, ALL, 0, 0, tiled=True)]
  transfers between devices with their start and end apart: 2 -> 5, of which waited for: 2 -> 2; matrix products, arithmetic and copies ran while one was open for 1% -> 0% of each run, Pallas kernels for 0% -> 45%
where the time goes in v2:
time: 114 us; the launch traced here: 113 us
  Pallas kernels  60.5 us (53%)
  blocking collectives  24.5 us (21%)
  starting transfers between devices  19.1 us (17%)
  waiting for transfers between devices  6.71 us (6%)
    pallas_call x2, Pallas kernels, solve(): pl.pallas_call(functools.partial(solve_kernel, kind), out_shape=[jax.Shap...  51.1 us
    all_to_all x1, blocking collectives, body(): mine = lax.all_to_all(shares, ALL, 0, 0, tiled=True)  24.5 us
    all_to_all x1, starting transfers between devices, body(): gathered = lax.all_to_all(sums, ALL, 0, 0, tiled=True)  15.3 us
    pallas_call x1, Pallas kernels, update(): pl.pallas_call(update_kernel, out_shape=[jax.ShapeDtypeStruct((ROWS, NNA)...  6.51 us
    all_to_all x1, waiting for transfers between devices, body(): gathered = lax.all_to_all(sums, ALL, 0, 0, tiled=True)  4.42 us
    pallas_call x1, Pallas kernels, average(): pl.pallas_call(average_kernel, out_shape=jax.ShapeDtypeStruct((GROUPS * N...  2.91 us
    ppermute x3, starting transfers between devices, body(): lax.ppermute(pdhg_counts, 'cyl', [(0, c)])  2.62 us
    ppermute x1, waiting for transfers between devices, body(): other = lax.ppermute(mine, 'cyl', [(0, 1), (1, 0), (2, 3), (3, 2)])  2.29 us
  transfers between devices with their start and end apart: 5, of which 2 were waited for; matrix products, arithmetic and copies ran while one was open for 0% of the time, Pallas kernels for 45%

profile of v2, /device:TPU:1, one launch (start us, length us, event | category | flops | bytes accessed | tf_op | source)
XLA Modules:
  0.0 112.8 jit_solution(13869145106413852133)
XLA Ops:
  0.6 0.7 collective-permute-start.1
  1.3 1.3 %collective-permute-start = (s32[1,64]{1,0:T(1,128)}, s32[1,64]{1,0:T(1,128)S(1)}, u32[]{:S(2)}, u32[]{:S(2)}) collective-permute-start(s32[1,64]{1,0:T(1,128)} %refs_3_.3), channel_id=1, source_target_pairs={{0,32},{1,33},{2,34},{3,35},{4,36},{5,37},{6,38},{7,39},{8,40},{9,... | collective-permute-start | bytes 776 | tf_op jit(solution)/shard_map/ppermute | solution.py:537
  2.6 0.7 collective-permute-start.2
  3.3 25.6 %solve_own.1 = (f32[1,64,20480]{2,1,0:T(8,128)}, f32[1,64,4096]{2,1,0:T(8,128)}, f32[128,32,128]{2,1,0:T(8,128)}) custom-call(s32[3,32]{1,0:T(4,128)} %bitcast.10, f32[4]{0:T(128)} %prox.3, s32[1,64]{1,0:T(1,128)} %bitcast.4, s32[1,64]{1,0:T(1,128)} %refs_3_.3, f32[64,20480]{1,0:T(8,128)} %refs_4_.3, f32[64,4096]{1,0:T(8,128)} %refs_5_.3, ...), custom_call_target="tpu_custom_call" | custom-call | flops 10000000000 | bytes 40000000 | tf_op jit(solution)/shard_map/solve_own/pallas_call | solution.py:350
  28.9 0.0 collective-permute-done.1.refs_14_
  28.9 0.0 copy-start.2
  28.9 0.0 collective-permute-done.refs_13_
  29.0 0.0 copy-start.3
  29.0 0.0 collective-permute-done.2.refs_15_
  29.0 0.0 copy-start.4
  29.0 15.3 %all-to-all-start = ((f32[128,32,128]{2,1,0:T(8,128)}), f32[128,32,128]{2,1,0:T(8,128)}, u32[]{:S(2)}, u32[]{:S(2)}) async-start(f32[128,32,128]{2,1,0:T(8,128)} %get-tuple-element.22), calls=%async_computation | async-start | bytes 4194304 | tf_op jit(solution)/shard_map/all_to_all | solution.py:544
  44.3 0.0 copy-done.2
  44.3 0.0 copy-done.3
  44.3 0.0 copy-done.4
  44.3 25.4 %solve_hub.1 = (f32[64,16384]{1,0:T(8,128)}, f32[8,128]{1,0:T(8,128)}) custom-call(s32[3,32]{1,0:T(4,128)} %bitcast.11, f32[4]{0:T(128)} %prox.3, s32[1,64]{1,0:T(1,128)} %bitcast.5, s32[1,64]{1,0:T(1,128)} %refs_3_.3, f32[64,20480]{1,0:T(8,128)} %refs_4_.3, f32[64,4096]{1,0:T(8,128)} %refs_5_.3, f32[64,16384]{1,0:T(8,128)} %refs_6_.3, f32[64,128]{1,0:T(8,128)} %bitcast.8, ...), custom_call_target="tpu_custom_call" | custom-call | flops 10000000000 | bytes 40000000 | tf_op jit(solution)/shard_map/solve_hub/pallas_call | solution.py:350
  69.8 4.4 %all-to-all-done.sums = f32[128,32,128]{2,1,0:T(8,128)} async-done(((f32[128,32,128]{2,1,0:T(8,128)}), f32[128,32,128]{2,1,0:T(8,128)}, u32[]{:S(2)}, u32[]{:S(2)}) %all-to-all-start) | async-done | bytes 2097184 | tf_op jit(solution)/shard_map/all_to_all | solution.py:544
  74.2 2.9 %average.1 = f32[128,16,128]{2,1,0:T(8,128)} custom-call(f32[4]{0:T(128)} %prox.3, f32[128,32,128]{2,1,0:T(8,128)} %all-to-all-done.sums, f32[8,128]{1,0:T(8,128)} %get-tuple-element.26.lagrange), custom_call_target="tpu_custom_call" | custom-call | flops 10000000 | bytes 4000000 | tf_op jit(solution)/shard_map/average/pallas_call | solution.py:418
  77.1 24.5 %all_to_all.10.mine = f32[128,16,128]{2,1,0:T(8,128)S(1)} all-to-all(f32[128,16,128]{2,1,0:T(8,128)} %average.1), channel_id=1, replica_groups=mesh['cyl'=4,'scen'=32] {'scen','cyl'}, dimensions={0} | all-to-all | bytes 2097152 | tf_op jit(solution)/shard_map/all_to_all | solution.py:547
  101.6 0.0 copy-start
  101.6 1.2 %collective-permute-start.3 = (f32[128,16,128]{2,1,0:T(8,128)S(1)}, f32[128,16,128]{2,1,0:T(8,128)S(1)}, u32[]{:S(2)}, u32[]{:S(2)}) collective-permute-start(f32[128,16,128]{2,1,0:T(8,128)S(1)} %all_to_all.10.mine), channel_id=1, source_target_pairs={{0,32},{32,0},{64,96},{96,64},{1,33},{33,1},{65,97},{97,65},{2,34}... | collective-permute-start | bytes 3145736 | tf_op jit(solution)/shard_map/ppermute | solution.py:548
  102.8 2.3 %collective-permute-done.3.other = f32[128,16,128]{2,1,0:T(8,128)S(1)} collective-permute-done((f32[128,16,128]{2,1,0:T(8,128)S(1)}, f32[128,16,128]{2,1,0:T(8,128)S(1)}, u32[]{:S(2)}, u32[]{:S(2)}) %collective-permute-start.3) | collective-permute-done | bytes 1048608 | tf_op jit(solution)/shard_map/ppermute | solution.py:548
  105.1 0.0 copy-start.1
  105.1 1.0 copy-done.1
  106.1 0.0 copy-done
  106.1 6.5 %update.1 = (f32[64,16384]{1,0:T(8,128)}, f32[64,128]{1,0:T(8,128)}, f32[48,8192]{1,0:T(8,128)}, f32[4]{0:T(128)}) custom-call(f32[4]{0:T(128)} %prox.3, f32[128,16,128]{2,1,0:T(8,128)} %copy-done, f32[128,16,128]{2,1,0:T(8,128)} %copy-done.1, f32[64,16384]{1,0:T(8,128)} %get-tuple-element.27.weights, s32[1,64]{1,0:T(1,128)} %bitcast.6), custom_call_target="tpu_custom_call" | custom-call | flops 1000000000 | bytes 20000000 | tf_op jit(solution)/shard_map/update/pallas_call | solution.py:500
Async XLA Ops:
  0.6 28.3 %collective-permute-start.1 = (s32[1,64]{1,0:T(1,128)}, s32[1,64]{1,0:T(1,128)S(1)}, u32[]{:S(2)}, u32[]{:S(2)}) collective-permute-start(s32[1,64]{1,0:T(1,128)} %refs_3_.3), channel_id=1, source_target_pairs={{0,64},{1,65},{2,66},{3,67},{4,68},{5,69},{6,70},{7,71},{8,72},{9,... | collective-permute-start | bytes 776 | tf_op jit(solution)/shard_map/ppermute | solution.py:537
  1.3 27.7 %collective-permute-start = (s32[1,64]{1,0:T(1,128)}, s32[1,64]{1,0:T(1,128)S(1)}, u32[]{:S(2)}, u32[]{:S(2)}) collective-permute-start(s32[1,64]{1,0:T(1,128)} %refs_3_.3), channel_id=1, source_target_pairs={{0,32},{1,33},{2,34},{3,35},{4,36},{5,37},{6,38},{7,39},{8,40},{9,... | collective-permute-start | bytes 776 | tf_op jit(solution)/shard_map/ppermute | solution.py:537
  2.6 26.4 %collective-permute-start.2 = (s32[1,64]{1,0:T(1,128)}, s32[1,64]{1,0:T(1,128)S(1)}, u32[]{:S(2)}, u32[]{:S(2)}) collective-permute-start(s32[1,64]{1,0:T(1,128)} %refs_3_.3), channel_id=1, source_target_pairs={{0,96},{1,97},{2,98},{3,99},{4,100},{5,101},{6,102},{7,103},{8,104... | collective-permute-start | bytes 776 | tf_op jit(solution)/shard_map/ppermute | solution.py:537
  28.9 15.4 %copy-start.2 = (s32[1,64]{1,0:T(1,128)}, s32[1,64]{1,0:T(1,128)S(1)}, u32[]{:S(2)}) copy-start(s32[1,64]{1,0:T(1,128)S(1)} %collective-permute-done.1.refs_14_) | copy-start | bytes 772
  29.0 15.4 %copy-start.3 = (s32[1,64]{1,0:T(1,128)}, s32[1,64]{1,0:T(1,128)S(1)}, u32[]{:S(2)}) copy-start(s32[1,64]{1,0:T(1,128)S(1)} %collective-permute-done.refs_13_) | copy-start | bytes 772
  29.0 15.3 %copy-start.4 = (s32[1,64]{1,0:T(1,128)}, s32[1,64]{1,0:T(1,128)S(1)}, u32[]{:S(2)}) copy-start(s32[1,64]{1,0:T(1,128)S(1)} %collective-permute-done.2.refs_15_) | copy-start | bytes 772
  29.0 45.2 %all-to-all-start = ((f32[128,32,128]{2,1,0:T(8,128)}), f32[128,32,128]{2,1,0:T(8,128)}, u32[]{:S(2)}, u32[]{:S(2)}) async-start(f32[128,32,128]{2,1,0:T(8,128)} %get-tuple-element.22), calls=%async_computation | async-start | bytes 4194304 | tf_op jit(solution)/shard_map/all_to_all | solution.py:544
  101.6 4.5 %copy-start = (f32[128,16,128]{2,1,0:T(8,128)}, f32[128,16,128]{2,1,0:T(8,128)S(1)}, u32[]{:S(2)}) copy-start(f32[128,16,128]{2,1,0:T(8,128)S(1)} %all_to_all.10.mine) | copy-start | bytes 3145732
  101.6 3.5 %collective-permute-start.3 = (f32[128,16,128]{2,1,0:T(8,128)S(1)}, f32[128,16,128]{2,1,0:T(8,128)S(1)}, u32[]{:S(2)}, u32[]{:S(2)}) collective-permute-start(f32[128,16,128]{2,1,0:T(8,128)S(1)} %all_to_all.10.mine), channel_id=1, source_target_pairs={{0,32},{32,0},{64,96},{96,64},{1,33},{33,1},{65,97},{97,65},{2,34}... | collective-permute-start | bytes 3145736 | tf_op jit(solution)/shard_map/ppermute | solution.py:548
  105.1 1.0 copy-start.1

commit v3 on v2

--- a/solution.py
+++ b/solution.py
@@ -68,8 +68,8 @@
     refs = refs[11:]
     is_hub = kind == "hub"
     if is_hub:
-        (blocks, own_in, first_counts, second_counts, third_counts, weights, lagrange) = refs[:7]
-        refs = refs[7:]
+        (blocks, own_in, weights, lagrange) = refs[:4]
+        refs = refs[4:]
     else:
         blocks, primal, dual, sums = refs[:4]
         refs = refs[4:]
@@ -78,6 +78,15 @@
         counts, z, z_odd, z_own, z_free, d, gc, gm, back, back_odd, ext, ext_own, u, uq, rh, wide, tall, nodes, firsts,
         extra, sem, osem,
     ) = (*refs[:26], refs[26:-2], *refs[-2:])
+    extra, small, head_smem = extra[:-3], extra[-3:-1], extra[-1]
+    pattern_copy = pltpu.make_async_copy(pattern, head_smem, sem.at[52])
+    small_copies = [
+        pltpu.make_async_copy(node_of, small[0], sem.at[53]),
+        pltpu.make_async_copy(counts_in.at[pl.ds(0, 1)], small[1], sem.at[54]),
+    ]
+    for one in [pattern_copy, *small_copies]:
+        one.start()
+    pattern = head_smem
     cyl = lax.axis_index("cyl")
     rho = prox[0] if is_hub else prox[cyl]
     inv = jnp.broadcast_to((1.0 / (1.0 + TAU * jnp.full((8, BLK), rho, jnp.float32)))[:1], (ROWS, BLK))
@@ -117,6 +126,8 @@
         own_copy = copy(own_in.at[0], extra[0], 0)
         own_copy.start()
 
+    pattern_copy.wait()
+
     def clear(c, carry):
         lead_of[c] = -1
         return carry
@@ -154,12 +165,10 @@
         return carry
 
     lax.fori_loop(used, 64, fill, 0)
-    if is_hub:
-        mine = jnp.where(cyl == 0, counts_in[...], 0)
-        counts[...] = down(mine + first_counts[...] + second_counts[...] + third_counts[...])
-    else:
-        counts[...] = down(counts_in[...])
-    hot = one_hot(node_of[...])
+    for one in small_copies:
+        one.wait()
+    counts[...] = down(small[1][...].reshape(1, ROWS))
+    hot = one_hot(small[0][...])
     hot_low = hot.astype(jnp.bfloat16)[:, :NODES]
     hot_turned = hot.T[:NODES].astype(jnp.bfloat16)
 
@@ -343,14 +352,14 @@
     shares = (GROUPS * N_CYL, SHARD, BLK)
     if kind == "hub":
         outs = [((ROWS, NNA), f32), ((8, BLK), f32)]
-        extra, out_specs, in_more = [V((ROWS, NZ), f32)], [HBM, VM], [HBM, HBM] + [VM] * 3
+        extra, out_specs, in_more = [V((ROWS, NZ), f32)], [HBM, VM], [HBM, HBM]
     else:
         outs = [((1, ROWS, NZ), f32), ((1, ROWS, M), f32), (shares, f32)]
         extra, out_specs, in_more = [V(shares, f32)], [HBM] * 3, [HBM]
     return pl.pallas_call(
         functools.partial(solve_kernel, kind),
         out_shape=[jax.ShapeDtypeStruct(*one) for one in outs],
-        in_specs=[SM, SM, VM, VM] + [HBM] * 7 + in_more,
+        in_specs=[HBM, SM, HBM, HBM] + [HBM] * 7 + in_more,
         out_specs=out_specs,
         scratch_shapes=[
             *[pltpu.SMEM((136,), i32)] * 7,
@@ -374,7 +383,10 @@
             V((NODES, N2), f32),
             V((CB1, BLK), f32),
             *extra,
-            pltpu.SemaphoreType.DMA((56,)),
+            V((1, ROWS), i32),
+            V((1, 1, ROWS), i32),
+            pltpu.SMEM((3, RB), i32),
+            pltpu.SemaphoreType.DMA((60,)),
             pltpu.SemaphoreType.DMA((8,)),
         ],
         compiler_params=pltpu.CompilerParams(vmem_limit_bytes=VMEM_LIMIT),
@@ -514,7 +526,7 @@
             pltpu.SemaphoreType.DMA((12,)),
             pltpu.SemaphoreType.DMA((12,)),
         ],
-        compiler_params=pltpu.CompilerParams(vmem_limit_bytes=VMEM_LIMIT),
+        compiler_params=pltpu.CompilerParams(vmem_limit_bytes=32 * 2**20),
         cost_estimate=pl.CostEstimate(flops=10**9, bytes_accessed=2 * 10**7, transcendentals=0),
         name="update",
     )(prox, mine, other, weights, node_of)
@@ -534,15 +546,16 @@
     node_of,
     pdhg_counts,
 ):
-    hub_counts = [lax.ppermute(pdhg_counts, "cyl", [(0, c)]) for c in range(1, N_CYL)]
+    own_counts = pdhg_counts.reshape(1, 1, ROWS)
+    all_counts = lax.all_to_all(jnp.broadcast_to(own_counts, (N_CYL, 1, ROWS)), "cyl", 0, 0, tiled=True)
     pattern = block_pattern.T
     node_row = node_of.reshape(1, ROWS)
     data = (costs, rhs, multipliers, xbar_first_in.reshape(CB1, BLK), xbar_node_in, start_primal, start_dual)
-    ints = (pattern, prox_weights, node_row, pdhg_counts)
-    primal, dual, sums = solve("own", *ints, *data, recourse_blocks)
-    sums, *hub_counts = lax.optimization_barrier((sums, *hub_counts))
+    ints = (pattern, prox_weights, node_row)
+    primal, dual, sums = solve("own", *ints, own_counts, *data, recourse_blocks)
+    sums, all_counts = lax.optimization_barrier((sums, all_counts))
     gathered = lax.all_to_all(sums, ALL, 0, 0, tiled=True)
-    weights, lagrange = solve("hub", *ints, *data, recourse_blocks, primal, *hub_counts)
+    weights, lagrange = solve("hub", *ints, all_counts, *data, recourse_blocks, primal)
     shares = average(prox_weights, gathered, lagrange)
     mine = lax.all_to_all(shares, ALL, 0, 0, tiled=True)
     other = lax.ppermute(mine, "cyl", [(0, 1), (1, 0), (2, 3), (3, 2)])

time: 114 us -> 112 us (0.982); the launches traced: 113 us -> 112 us
  local copies, waits for them, and re-layouts: 1.02 us -> 3.44 us
  starting transfers between devices: 19.1 us -> 16.7 us
    all_to_all x0 -> x1, starting transfers between devices: none -> 4.69 us  [body(): lax.all_to_all(jnp.broadcast_to(own_counts, (N_CYL, 1, ROWS)), 'cyl', 0,...]
    all_to_all x1, starting transfers between devices: 15.3 us -> 10.9 us  [body(): gathered = lax.all_to_all(sums, ALL, 0, 0, tiled=True)]
    ppermute x3 -> x0, starting transfers between devices: 2.62 us -> none  [body(): lax.ppermute(pdhg_counts, 'cyl', [(0, c)])]
    pallas_call x1, Pallas kernels: 6.51 us -> 5.06 us  [update(): pl.pallas_call(update_kernel, out_shape=[jax.ShapeDtypeStruct((ROWS, NNA)...]
    broadcast_in_dim x0 -> x1, local copies, waits for them, and re-layouts: none -> 1.24 us  [body(): jnp.broadcast_to(own_counts, (N_CYL, 1, ROWS))]
    unnamed x10 -> x8, local copies, waits for them, and re-layouts: 1.02 us -> 2.21 us
  transfers between devices with their start and end apart: 5 -> 3, of which waited for: 2 -> 2; matrix products, arithmetic and copies ran while one was open for 0% -> 0% of each run, Pallas kernels for 45% -> 46%
where the time goes in v3:
time: 112 us
  Pallas kernels  59.7 us (53%)
  blocking collectives  24.8 us (22%)
  starting transfers between devices  16.7 us (15%)
  waiting for transfers between devices  6.43 us (6%)
  local copies, waits for them, and re-layouts  3.44 us (3%)
    pallas_call x2, Pallas kernels, solve(): pl.pallas_call(functools.partial(solve_kernel, kind), out_shape=[jax.Shap...  51.7 us
    all_to_all x1, blocking collectives, body(): mine = lax.all_to_all(shares, ALL, 0, 0, tiled=True)  24.8 us
    all_to_all x1, starting transfers between devices, body(): gathered = lax.all_to_all(sums, ALL, 0, 0, tiled=True)  10.9 us
    pallas_call x1, Pallas kernels, update(): pl.pallas_call(update_kernel, out_shape=[jax.ShapeDtypeStruct((ROWS, NNA)...  5.06 us
    all_to_all x1, starting transfers between devices, body(): lax.all_to_all(jnp.broadcast_to(own_counts, (N_CYL, 1, ROWS)), 'cyl', 0,...  4.69 us
    all_to_all x1, waiting for transfers between devices, body(): gathered = lax.all_to_all(sums, ALL, 0, 0, tiled=True)  4.14 us
    pallas_call x1, Pallas kernels, average(): pl.pallas_call(average_kernel, out_shape=jax.ShapeDtypeStruct((GROUPS * N...  2.91 us
    ppermute x1, waiting for transfers between devices, body(): other = lax.ppermute(mine, 'cyl', [(0, 1), (1, 0), (2, 3), (3, 2)])  2.29 us
  transfers between devices with their start and end apart: 3, of which 2 were waited for; matrix products, arithmetic and copies ran while one was open for 0% of the time, Pallas kernels for 46%

profile of v3, /device:TPU:1, one launch (start us, length us, event | category | flops | bytes accessed | tf_op | source)
XLA Modules:
  0.0 112.0 jit_solution(8897913942476382274)
XLA Ops:
  0.6 1.2 %broadcast_in_dim.8 = s32[4,1,64]{2,1,0:T(1,128)} broadcast(s32[64]{0:T(128)} %bitcast.9), dimensions={2} | broadcast | bytes 1280 | tf_op jit(solution)/shard_map/broadcast_in_dim | solution.py:550
  1.9 4.7 %all-to-all-start = ((s32[4,1,64]{2,1,0:T(1,128)}), s32[4,1,64]{2,1,0:T(1,128)S(1)}, u32[]{:S(2)}, u32[]{:S(2)}) async-start(s32[4,1,64]{2,1,0:T(1,128)} %broadcast_in_dim.8), calls=%async_computation | async-start | bytes 4096 | tf_op jit(solution)/shard_map/all_to_all | solution.py:550
  6.6 26.0 %solve_own.1 = (f32[1,64,20480]{2,1,0:T(8,128)}, f32[1,64,4096]{2,1,0:T(8,128)}, f32[128,32,128]{2,1,0:T(8,128)}) custom-call(s32[3,32]{1,0:T(4,128)} %bitcast.14, f32[4]{0:T(128)} %prox.3, s32[1,64]{1,0:T(1,128)} %bitcast.6, s32[1,1,64]{2,1,0:T(1,128)} %bitcast.10, f32[64,20480]{1,0:T(8,128)} %refs_4_.3, f32[64,4096]{1,0:T(8,128)} %refs_5_.3, ...), custom_call_target="tpu_custom_call" | custom-call | flops 10000000000 | bytes 40000000 | tf_op jit(solution)/shard_map/solve_own/pallas_call | solution.py:359
  32.6 0.0 all-to-all-done.refs_3_
  32.6 0.0 copy-start.3
  32.6 10.9 %all-to-all-start.1 = ((f32[128,32,128]{2,1,0:T(8,128)}), f32[128,32,128]{2,1,0:T(8,128)}, u32[]{:S(2)}, u32[]{:S(2)}) async-start(f32[128,32,128]{2,1,0:T(8,128)} %get-tuple-element.20), calls=%async_computation.1 | async-start | bytes 4194304 | tf_op jit(solution)/shard_map/all_to_all | solution.py:557
  43.5 0.0 copy-done.3
  43.5 25.7 %solve_hub.1 = (f32[64,16384]{1,0:T(8,128)}, f32[8,128]{1,0:T(8,128)}) custom-call(s32[3,32]{1,0:T(4,128)} %bitcast.15, f32[4]{0:T(128)} %prox.3, s32[1,64]{1,0:T(1,128)} %bitcast.7, s32[4,1,64]{2,1,0:T(1,128)} %copy-done.3, f32[64,20480]{1,0:T(8,128)} %refs_4_.3, f32[64,4096]{1,0:T(8,128)} %refs_5_.3, f32[64,16384]{1,0:T(8,128)} %refs_6_.3, ...), custom_call_target="tpu_custom_call" | custom-call | flops 10000000000 | bytes 40000000 | tf_op jit(solution)/shard_map/solve_hub/pallas_call | solution.py:359
  69.2 0.0 copy-start.1
  69.2 0.0 copy-start.2
  69.2 4.1 %all-to-all-done.1.sums = f32[128,32,128]{2,1,0:T(8,128)} async-done(((f32[128,32,128]{2,1,0:T(8,128)}), f32[128,32,128]{2,1,0:T(8,128)}, u32[]{:S(2)}, u32[]{:S(2)}) %all-to-all-start.1) | async-done | bytes 2097184 | tf_op jit(solution)/shard_map/all_to_all | solution.py:557
  73.4 2.9 %average.1 = f32[128,16,128]{2,1,0:T(8,128)} custom-call(f32[4]{0:T(128)} %prox.3, f32[128,32,128]{2,1,0:T(8,128)} %all-to-all-done.1.sums, f32[8,128]{1,0:T(8,128)} %get-tuple-element.22.lagrange), custom_call_target="tpu_custom_call" | custom-call | flops 10000000 | bytes 4000000 | tf_op jit(solution)/shard_map/average/pallas_call | solution.py:430
  76.3 24.8 %all_to_all.15.mine = f32[128,16,128]{2,1,0:T(8,128)S(1)} all-to-all(f32[128,16,128]{2,1,0:T(8,128)} %average.1), channel_id=1, replica_groups=mesh['cyl'=4,'scen'=32] {'scen','cyl'}, dimensions={0} | all-to-all | bytes 2097152 | tf_op jit(solution)/shard_map/all_to_all | solution.py:560
  101.1 1.2 %collective-permute-start = (f32[128,16,128]{2,1,0:T(8,128)S(1)}, f32[128,16,128]{2,1,0:T(8,128)S(1)}, u32[]{:S(2)}, u32[]{:S(2)}) collective-permute-start(f32[128,16,128]{2,1,0:T(8,128)S(1)} %all_to_all.15.mine), channel_id=1, source_target_pairs={{0,32},{32,0},{64,96},{96,64},{1,33},{33,1},{65,97},{97,65},{2,34}... | collective-permute-start | bytes 3145736 | tf_op jit(solution)/shard_map/ppermute | solution.py:561
  102.3 2.3 %collective-permute-done.other = f32[128,16,128]{2,1,0:T(8,128)S(1)} collective-permute-done((f32[128,16,128]{2,1,0:T(8,128)S(1)}, f32[128,16,128]{2,1,0:T(8,128)S(1)}, u32[]{:S(2)}, u32[]{:S(2)}) %collective-permute-start) | collective-permute-done | bytes 1048608 | tf_op jit(solution)/shard_map/ppermute | solution.py:561
  104.6 0.0 copy-done.1
  104.6 0.0 copy-done.2
  104.6 0.0 copy-start
  104.6 2.2 %copy-done = f32[64,16384]{1,0:T(8,128)S(1)} copy-done((f32[64,16384]{1,0:T(8,128)S(1)}, f32[64,16384]{1,0:T(8,128)}, u32[]{:S(2)}) %copy-start) | copy-done | bytes 4194328
  106.8 5.1 %update.1 = (f32[64,16384]{1,0:T(8,128)}, f32[64,128]{1,0:T(8,128)}, f32[48,8192]{1,0:T(8,128)}, f32[4]{0:T(128)}) custom-call(f32[4]{0:T(128)S(1)} %copy-done.1, f32[128,16,128]{2,1,0:T(8,128)S(1)} %all_to_all.15.mine, f32[128,16,128]{2,1,0:T(8,128)S(1)} %collective-permute-done.other, f32[64,16384]{1,0:T(8,128)S(1)} %copy-done, s32[1,64]{1,0:T(1,128)S(1)} %bitcast.8), custom_call_target="tpu_custom_call" | custom-call | flops 1000000000 | bytes 20000000 | tf_op jit(solution)/shard_map/update/pallas_call | solution.py:512
Async XLA Ops:
  1.9 30.7 %all-to-all-start = ((s32[4,1,64]{2,1,0:T(1,128)}), s32[4,1,64]{2,1,0:T(1,128)S(1)}, u32[]{:S(2)}, u32[]{:S(2)}) async-start(s32[4,1,64]{2,1,0:T(1,128)} %broadcast_in_dim.8), calls=%async_computation | async-start | bytes 4096 | tf_op jit(solution)/shard_map/all_to_all | solution.py:550
  32.6 10.9 %copy-start.3 = (s32[4,1,64]{2,1,0:T(1,128)}, s32[4,1,64]{2,1,0:T(1,128)S(1)}, u32[]{:S(2)}) copy-start(s32[4,1,64]{2,1,0:T(1,128)S(1)} %all-to-all-done.refs_3_) | copy-start | bytes 3076
  32.6 40.8 %all-to-all-start.1 = ((f32[128,32,128]{2,1,0:T(8,128)}), f32[128,32,128]{2,1,0:T(8,128)}, u32[]{:S(2)}, u32[]{:S(2)}) async-start(f32[128,32,128]{2,1,0:T(8,128)} %get-tuple-element.20), calls=%async_computation.1 | async-start | bytes 4194304 | tf_op jit(solution)/shard_map/all_to_all | solution.py:557
  69.2 35.4 %copy-start.1 = (f32[4]{0:T(128)S(1)}, f32[4]{0:T(128)}, u32[]{:S(2)}) copy-start(f32[4]{0:T(128)} %prox.3) | copy-start | bytes 52
  69.2 35.4 %copy-start.2 = (s32[64]{0:T(128)S(1)}, s32[64]{0:T(128)}, u32[]{:S(2)}) copy-start(s32[64]{0:T(128)} %param.22) | copy-start | bytes 772
  101.1 3.5 %collective-permute-start = (f32[128,16,128]{2,1,0:T(8,128)S(1)}, f32[128,16,128]{2,1,0:T(8,128)S(1)}, u32[]{:S(2)}, u32[]{:S(2)}) collective-permute-start(f32[128,16,128]{2,1,0:T(8,128)S(1)} %all_to_all.15.mine), channel_id=1, source_target_pairs={{0,32},{32,0},{64,96},{96,64},{1,33},{33,1},{65,97},{97,65},{2,34}... | collective-permute-start | bytes 3145736 | tf_op jit(solution)/shard_map/ppermute | solution.py:561
  104.6 2.2 %copy-start = (f32[64,16384]{1,0:T(8,128)S(1)}, f32[64,16384]{1,0:T(8,128)}, u32[]{:S(2)}) copy-start(f32[64,16384]{1,0:T(8,128)} %get-tuple-element.23.weights) | copy-start | bytes 12582916

commit v4 on v3

--- a/solution.py
+++ b/solution.py
@@ -432,6 +432,7 @@
         out_shape=jax.ShapeDtypeStruct((GROUPS * N_CYL, SHARD // 2, BLK), jnp.float32),
         in_specs=[SM, VM, VM],
         out_specs=VM,
+        compiler_params=pltpu.CompilerParams(vmem_limit_bytes=32 * 2**20),
         cost_estimate=pl.CostEstimate(flops=10**7, bytes_accessed=4 * 10**6, transcendentals=0),
         name="average",
     )(prox, sums, lagrange)

time: 112 us -> 110 us (0.982)
  local copies, waits for them, and re-layouts: 3.44 us -> 2.1 us
    unnamed x8 -> x10, local copies, waits for them, and re-layouts: 2.21 us -> 0.86 us
  transfers between devices with their start and end apart: 3 -> 3, of which waited for: 2 -> 2; matrix products, arithmetic and copies ran while one was open for 0% -> 0% of each run, Pallas kernels for 46% -> 47%
where the time goes in v4:
time: 110 us
  Pallas kernels  59.1 us (54%)
  blocking collectives  24.8 us (23%)
  starting transfers between devices  16.7 us (15%)
  waiting for transfers between devices  6.29 us (6%)
  local copies, waits for them, and re-layouts  2.1 us (2%)
    pallas_call x2, Pallas kernels, solve(): pl.pallas_call(functools.partial(solve_kernel, kind), out_shape=[jax.Shap...  51.9 us
    all_to_all x1, blocking collectives, body(): mine = lax.all_to_all(shares, ALL, 0, 0, tiled=True)  24.8 us
    all_to_all x1, starting transfers between devices, body(): gathered = lax.all_to_all(sums, ALL, 0, 0, tiled=True)  10.9 us
    pallas_call x1, Pallas kernels, update(): pl.pallas_call(update_kernel, out_shape=[jax.ShapeDtypeStruct((ROWS, NNA)...  5.06 us
    all_to_all x1, starting transfers between devices, body(): lax.all_to_all(jnp.broadcast_to(own_counts, (N_CYL, 1, ROWS)), 'cyl', 0,...  4.69 us
    all_to_all x1, waiting for transfers between devices, body(): gathered = lax.all_to_all(sums, ALL, 0, 0, tiled=True)  4 us
    ppermute x1, waiting for transfers between devices, body(): other = lax.ppermute(mine, 'cyl', [(0, 1), (1, 0), (2, 3), (3, 2)])  2.29 us
  transfers between devices with their start and end apart: 3, of which 2 were waited for; matrix products, arithmetic and copies ran while one was open for 0% of the time, Pallas kernels for 47%

profile of v4, /device:TPU:1, one launch (start us, length us, event | category | flops | bytes accessed | tf_op | source)
XLA Modules:
  0.0 109.8 jit_solution(12505186996745564088)
XLA Ops:
  0.6 1.2 %broadcast_in_dim.8 = s32[4,1,64]{2,1,0:T(1,128)} broadcast(s32[64]{0:T(128)} %bitcast.9), dimensions={2} | broadcast | bytes 1280 | tf_op jit(solution)/shard_map/broadcast_in_dim | solution.py:551
  1.9 4.7 %all-to-all-start = ((s32[4,1,64]{2,1,0:T(1,128)}), s32[4,1,64]{2,1,0:T(1,128)S(1)}, u32[]{:S(2)}, u32[]{:S(2)}) async-start(s32[4,1,64]{2,1,0:T(1,128)} %broadcast_in_dim.8), calls=%async_computation | async-start | bytes 4096 | tf_op jit(solution)/shard_map/all_to_all | solution.py:551
  6.6 26.0 %solve_own.1 = (f32[1,64,20480]{2,1,0:T(8,128)}, f32[1,64,4096]{2,1,0:T(8,128)}, f32[128,32,128]{2,1,0:T(8,128)}) custom-call(s32[3,32]{1,0:T(4,128)} %bitcast.14, f32[4]{0:T(128)} %prox.3, s32[1,64]{1,0:T(1,128)} %bitcast.6, s32[1,1,64]{2,1,0:T(1,128)} %bitcast.10, f32[64,20480]{1,0:T(8,128)} %refs_4_.3, f32[64,4096]{1,0:T(8,128)} %refs_5_.3, ...), custom_call_target="tpu_custom_call" | custom-call | flops 10000000000 | bytes 40000000 | tf_op jit(solution)/shard_map/solve_own/pallas_call | solution.py:359
  32.6 0.0 all-to-all-done.refs_3_
  32.6 0.0 copy-start.4
  32.6 10.9 %all-to-all-start.1 = ((f32[128,32,128]{2,1,0:T(8,128)}), f32[128,32,128]{2,1,0:T(8,128)}, u32[]{:S(2)}, u32[]{:S(2)}) async-start(f32[128,32,128]{2,1,0:T(8,128)} %get-tuple-element.20), calls=%async_computation.1 | async-start | bytes 4194304 | tf_op jit(solution)/shard_map/all_to_all | solution.py:558
  43.5 0.0 copy-done.4
  43.5 0.0 copy-start.2
  43.5 0.0 copy-start.3
  43.5 25.8 %solve_hub.1 = (f32[64,16384]{1,0:T(8,128)}, f32[8,128]{1,0:T(8,128)}) custom-call(s32[3,32]{1,0:T(4,128)} %bitcast.15, f32[4]{0:T(128)} %prox.3, s32[1,64]{1,0:T(1,128)} %bitcast.7, s32[4,1,64]{2,1,0:T(1,128)} %copy-done.4, f32[64,20480]{1,0:T(8,128)} %refs_4_.3, f32[64,4096]{1,0:T(8,128)} %refs_5_.3, f32[64,16384]{1,0:T(8,128)} %refs_6_.3, ...), custom_call_target="tpu_custom_call" | custom-call | flops 10000000000 | bytes 40000000 | tf_op jit(solution)/shard_map/solve_hub/pallas_call | solution.py:359
  69.4 4.0 %all-to-all-done.1.sums = f32[128,32,128]{2,1,0:T(8,128)} async-done(((f32[128,32,128]{2,1,0:T(8,128)}), f32[128,32,128]{2,1,0:T(8,128)}, u32[]{:S(2)}, u32[]{:S(2)}) %all-to-all-start.1) | async-done | bytes 2097184 | tf_op jit(solution)/shard_map/all_to_all | solution.py:558
  73.4 0.0 copy-start
  73.4 0.0 copy-done.2
  73.4 0.0 copy-start.1
  73.4 0.8 copy-done.1
  74.2 2.1 %average.1 = f32[128,16,128]{2,1,0:T(8,128)S(1)} custom-call(f32[4]{0:T(128)S(1)} %copy-done.2, f32[128,32,128]{2,1,0:T(8,128)} %all-to-all-done.1.sums, f32[8,128]{1,0:T(8,128)S(1)} %copy-done.1), custom_call_target="tpu_custom_call" | custom-call | flops 10000000 | bytes 4000000 | tf_op jit(solution)/shard_map/average/pallas_call | solution.py:430
  76.4 24.8 %all_to_all.15.mine = f32[128,16,128]{2,1,0:T(8,128)S(1)} all-to-all(f32[128,16,128]{2,1,0:T(8,128)S(1)} %average.1), channel_id=1, replica_groups=mesh['cyl'=4,'scen'=32] {'scen','cyl'}, dimensions={0} | all-to-all | bytes 2097152 | tf_op jit(solution)/shard_map/all_to_all | solution.py:561
  101.1 1.2 %collective-permute-start = (f32[128,16,128]{2,1,0:T(8,128)S(1)}, f32[128,16,128]{2,1,0:T(8,128)S(1)}, u32[]{:S(2)}, u32[]{:S(2)}) collective-permute-start(f32[128,16,128]{2,1,0:T(8,128)S(1)} %all_to_all.15.mine), channel_id=1, source_target_pairs={{0,32},{32,0},{64,96},{96,64},{1,33},{33,1},{65,97},{97,65},{2,34}... | collective-permute-start | bytes 3145736 | tf_op jit(solution)/shard_map/ppermute | solution.py:562
  102.3 2.3 %collective-permute-done.other = f32[128,16,128]{2,1,0:T(8,128)S(1)} collective-permute-done((f32[128,16,128]{2,1,0:T(8,128)S(1)}, f32[128,16,128]{2,1,0:T(8,128)S(1)}, u32[]{:S(2)}, u32[]{:S(2)}) %collective-permute-start) | collective-permute-done | bytes 1048608 | tf_op jit(solution)/shard_map/ppermute | solution.py:562
  104.6 0.0 copy-done.3
  104.6 0.0 copy-done
  104.6 5.1 %update.1 = (f32[64,16384]{1,0:T(8,128)}, f32[64,128]{1,0:T(8,128)}, f32[48,8192]{1,0:T(8,128)}, f32[4]{0:T(128)}) custom-call(f32[4]{0:T(128)S(1)} %copy-done.2, f32[128,16,128]{2,1,0:T(8,128)S(1)} %all_to_all.15.mine, f32[128,16,128]{2,1,0:T(8,128)S(1)} %collective-permute-done.other, f32[64,16384]{1,0:T(8,128)S(1)} %copy-done, s32[1,64]{1,0:T(1,128)S(1)} %bitcast.8), custom_call_target="tpu_custom_call" | custom-call | flops 1000000000 | bytes 20000000 | tf_op jit(solution)/shard_map/update/pallas_call | solution.py:513
Async XLA Ops:
  1.9 30.7 %all-to-all-start = ((s32[4,1,64]{2,1,0:T(1,128)}), s32[4,1,64]{2,1,0:T(1,128)S(1)}, u32[]{:S(2)}, u32[]{:S(2)}) async-start(s32[4,1,64]{2,1,0:T(1,128)} %broadcast_in_dim.8), calls=%async_computation | async-start | bytes 4096 | tf_op jit(solution)/shard_map/all_to_all | solution.py:551
  32.6 10.9 %copy-start.4 = (s32[4,1,64]{2,1,0:T(1,128)}, s32[4,1,64]{2,1,0:T(1,128)S(1)}, u32[]{:S(2)}) copy-start(s32[4,1,64]{2,1,0:T(1,128)S(1)} %all-to-all-done.refs_3_) | copy-start | bytes 3076
  32.6 40.8 %all-to-all-start.1 = ((f32[128,32,128]{2,1,0:T(8,128)}), f32[128,32,128]{2,1,0:T(8,128)}, u32[]{:S(2)}, u32[]{:S(2)}) async-start(f32[128,32,128]{2,1,0:T(8,128)} %get-tuple-element.20), calls=%async_computation.1 | async-start | bytes 4194304 | tf_op jit(solution)/shard_map/all_to_all | solution.py:558
  43.5 29.9 %copy-start.2 = (f32[4]{0:T(128)S(1)}, f32[4]{0:T(128)}, u32[]{:S(2)}) copy-start(f32[4]{0:T(128)} %prox.3) | copy-start | bytes 52
  43.5 61.1 %copy-start.3 = (s32[64]{0:T(128)S(1)}, s32[64]{0:T(128)}, u32[]{:S(2)}) copy-start(s32[64]{0:T(128)} %param.22) | copy-start | bytes 772
  73.4 31.2 %copy-start = (f32[64,16384]{1,0:T(8,128)S(1)}, f32[64,16384]{1,0:T(8,128)}, u32[]{:S(2)}) copy-start(f32[64,16384]{1,0:T(8,128)} %get-tuple-element.23.weights) | copy-start | bytes 12582916
  73.4 0.8 copy-start.1
  101.1 3.5 %collective-permute-start = (f32[128,16,128]{2,1,0:T(8,128)S(1)}, f32[128,16,128]{2,1,0:T(8,128)S(1)}, u32[]{:S(2)}, u32[]{:S(2)}) collective-permute-start(f32[128,16,128]{2,1,0:T(8,128)S(1)} %all_to_all.15.mine), channel_id=1, source_target_pairs={{0,32},{32,0},{64,96},{96,64},{1,33},{33,1},{65,97},{97,65},{2,34}... | collective-permute-start | bytes 3145736 | tf_op jit(solution)/shard_map/ppermute | solution.py:562
